TPU v7x, 256 devices: a whole 4x4x8 slice. The times are simulated.
256 devices in a mesh: ctx: 32 (over y, z), head: 2 (over x_hi), inst: 4 (over x_lo, core).
Axes of the slice: x: 4 (x_hi: 2, x_lo: 2; x = x_hi * 2 + x_lo), y: 4, z: 8, core: 2. Of those that a mesh axis runs over, the one named last changes fastest.
Arguments:
- queries: bfloat16 [4096, 8, 8, 128], P('ctx', ('head', 'inst')), may hold values from -8 to 8
- cache_kv: bfloat16 [16384, 2, 8, 128], P('ctx', None, ('head', 'inst')), may hold values from -12 to 12
- new_kv: bfloat16 [4096, 2, 8, 128], P('ctx', None, ('head', 'inst')), may hold values from -12 to 12
- cache_lengths: int32 [32], replicated, may hold values from 64 to 512, as said below
- plan: int32 [256, 1], P('ctx'), may hold values from 0 to 3; in each aligned block of 8 rows (0 to 7, 8 to 15, ...) at most 4 rows name the same one
Outputs:
- attended: bfloat16 [4096, 8, 8, 128], P('ctx', ('head', 'inst'))
- migrated: bfloat16 [4, 32, 4, 16, 2, 8, 128], P('inst', 'ctx', 'head')
Inputs may be any that keep to these rules, and one draw needn't show every extreme that they name: Shard i's usable slots are its first cache_lengths[i]; some shard is full. `plan`: in the pages of one index of ctx (aligned blocks of 8 rows) no instance is named more than 4 times.
All inputs are finite; a program needn't handle non-finite values.
Results may differ from a plain program's by a relative error of at most 0.006.
Values may be sent and summed in bfloat16 or wider, within the bound.
A program may use at most 64 MiB of HBM per device.

v0:
```python
import jax
import jax.numpy as jnp
from jax import lax
from jax.sharding import PartitionSpec as P

BLOCK = 16


masked_score = -1e30


def shard_length(cache_lengths, shard_id):
    return jnp.sum(jnp.where(jnp.arange(cache_lengths.shape[0]) == shard_id, cache_lengths, 0))


def attend(softmax_state, query_mat, query_pos, kv_rows, cache_span, shard_id, length, tok_rows):
    running_max, running_sum, weighted = softmax_state
    key_rows = kv_rows[:, 0, :]
    value_rows = kv_rows[:, 1, :]
    scores = jnp.einsum(
        "qd,kd->qk", query_mat, key_rows, preferred_element_type=jnp.float32
    ) * query_mat.shape[1] ** (-0.5)
    positions = jnp.arange(kv_rows.shape[0])
    in_cache = positions < cache_span
    usable = jnp.where(
        in_cache[None, :],
        (positions < length)[None, :],
        (shard_id * tok_rows + positions - cache_span)[None, :] <= query_pos[:, None],
    )
    block_max = jnp.max(jnp.where(usable, scores, masked_score), axis=1)
    new_max = jnp.maximum(running_max, block_max)
    factor = jnp.exp(running_max - new_max)
    weights = jnp.where(usable, jnp.exp(scores - new_max[:, None]), 0.0)
    running_sum = running_sum * factor + jnp.sum(weights, axis=1)
    weighted = weighted * factor[:, None] + jnp.dot(
        weights.astype(jnp.bfloat16), value_rows, preferred_element_type=jnp.float32
    )
    return (new_max, running_sum, weighted)


def attention(queries, cache_kv, new_kv, cache_lengths):
    tok_rows = queries.shape[0]
    group_size = queries.shape[2]
    head_dim = queries.shape[3]
    cache_span = cache_kv.shape[0]
    kv_span = cache_span + tok_rows
    ctx_index = lax.axis_index("ctx")
    query_mat = queries.reshape(tok_rows * group_size, head_dim)
    local_kv = jnp.concatenate([cache_kv[:, :, 0, :], new_kv[:, :, 0, :]], axis=0)
    head_rows = tok_rows * group_size
    empty_state = (
        jnp.full((head_rows,), masked_score, jnp.float32),
        jnp.zeros((head_rows,), jnp.float32),
        jnp.zeros((head_rows, head_dim), jnp.float32),
    )
    query_pos = ctx_index * tok_rows + jnp.arange(head_rows) // group_size
    arrived_rows = lax.all_gather(local_kv, "ctx", axis=0, tiled=True)
    shard_count = arrived_rows.shape[0] // kv_span
    stacked = arrived_rows.reshape(shard_count, kv_span, 2, head_dim)

    def visit(carry_state, scan_input):
        kv_block, offset = scan_input
        return (
            attend(
                carry_state,
                query_mat,
                query_pos,
                kv_block,
                cache_span,
                offset,
                shard_length(cache_lengths, offset),
                tok_rows,
            ),
            None,
        )

    final_state, unused = lax.scan(
        visit, empty_state, (stacked, jnp.arange(shard_count, dtype=jnp.int32))
    )
    running_sum = final_state[1]
    weighted = final_state[2]
    result = (weighted / running_sum[:, None]).astype(jnp.bfloat16)
    return result.reshape(tok_rows, 1, group_size, head_dim)


def relocate(new_kv, plan):
    tok_rows = new_kv.shape[0]
    head_dim = new_kv.shape[3]
    inst_count = lax.axis_size("inst")
    head_count = lax.axis_size("head")
    blocks_here = tok_rows // BLOCK
    capacity = blocks_here // 2
    destination = plan[:, 0]
    block_order = jnp.arange(blocks_here)
    earlier = (block_order[:, None] < block_order[None, :]) & (
        destination[:, None] == destination[None, :]
    )
    slot_index = jnp.sum(earlier.astype(jnp.int32), axis=0)
    target = destination * capacity + slot_index
    select = (jnp.arange(inst_count * capacity)[:, None] == target[None, :]).astype(jnp.bfloat16)
    page_rows = new_kv.reshape(blocks_here, BLOCK * 2 * head_dim)
    packed = jnp.dot(select, page_rows, preferred_element_type=jnp.float32).astype(jnp.bfloat16)
    packed = packed.reshape(inst_count, capacity, BLOCK, 2, 1, head_dim)
    arrived = lax.all_to_all(
        lax.all_to_all(packed, "head", split_axis=1, concat_axis=4, tiled=True),
        "inst",
        split_axis=0,
        concat_axis=4,
        tiled=True,
    )
    part_slots = capacity // head_count
    arrived = arrived.reshape(part_slots, BLOCK, 2, inst_count, head_count, head_dim)
    arrived = jnp.swapaxes(arrived, 3, 4)
    return arrived.reshape(1, 1, part_slots, BLOCK, 2, inst_count * head_count, head_dim)


def body(queries, cache_kv, new_kv, cache_lengths, plan):
    attended = attention(queries, cache_kv, new_kv, cache_lengths)
    migrated = relocate(new_kv, plan)
    return (attended, migrated)


def solution(mesh):
    return jax.shard_map(
        body,
        mesh=mesh,
        in_specs=(
            P("ctx", ("head", "inst"), None, None),
            P("ctx", None, ("head", "inst"), None),
            P("ctx", None, ("head", "inst"), None),
            P(),
            P("ctx", None),
        ),
        out_specs=(
            P("ctx", ("head", "inst"), None, None),
            P("inst", "ctx", "head", None, None, None, None),
        ),
        check_vma=False,
    )
```

profile of v0, /device:TPU:1, one launch (start us, length us, event | category | flops | bytes accessed | tf_op | source)
XLA Modules:
  0.0 403.6 jit_solution(3837150768410154451)
XLA Ops:
  12.5 9.5 %all_to_all.33 = bf16[4,4,16,2,1,128]{5,3,2,0,4,1:T(2,128)(2,1)S(1)} all-to-all(bf16[4,4,16,2,1,128]{5,3,2,0,4,1:T(2,128)(2,1)S(1)} %copy.28), channel_id=1, replica_groups=mesh['ctx'=32,'head'=2,'inst'=4] {'head'}, dimensions={1} | all-to-all | bytes 262144 | tf_op jit(solution)/shard_map/all_to_all | solution.py:105
  22.9 5.4 %all-to-all-start.1 = ((bf16[4,2,16,2,2,128]{5,4,3,2,1,0:T(2,128)(2,1)}), bf16[4,2,16,2,2,128]{5,4,3,2,1,0:T(2,128)(2,1)S(1)}, u32[]{:S(2)}, u32[]{:S(2)}) async-start(bf16[4,2,16,2,2,128]{5,4,3,2,1,0:T(2,128)(2,1)} %bitcast.58), calls=%async_computation.1 | async-start | bytes 262144 | tf_op jit(solution)/shard_map/all_to_all | solution.py:104
  28.3 4.0 all-to-all-done.1
  33.0 90.2 %all-gather.2.cloned.1.call-done = bf16[20480,2,128]{2,0,1:T(8,128)(2,1)} async-done(((bf16[640,2,128]{2,0,1:T(8,128)(2,1)}), bf16[20480,2,128]{2,0,1:T(8,128)(2,1)}) %all-gather.2.cloned.1.call-update) | async-done | bytes 10485776 | tf_op jit(solution)/shard_map/all_gather | solution.py:57
  123.2 272.6 %while.17 = (s32[]{:T(128)}, f32[1024]{0:T(1024)S(1)}, f32[1024]{0:T(1024)S(1)}, f32[1024,128]{1,0:T(8,128)S(1)}, s32[32]{0:T(128)S(1)}, /*index=5*/s32[32]{0:T(...) while((s32[]{:T(128)}, f32[1024]{0:T(1024)S(1)}, ...), condition=%wide.region_4.5_spmd.clone, body=%wide.region_0.4_spmd.clone.sunk | while | flops 347095648 | bytes 10260273 | solution.py:77
  127.4 1.8 fusion.38
  144.4 1.8 fusion.38
  152.9 1.8 fusion.38
  161.5 1.8 fusion.38
  170.0 1.8 fusion.38
  178.5 1.8 fusion.38
  187.0 1.8 fusion.38
  195.5 1.8 fusion.38
  204.0 1.8 fusion.38
  212.6 1.8 fusion.38
  221.1 1.8 fusion.38
  229.6 1.8 fusion.38
  238.1 1.8 fusion.38
  246.6 1.8 fusion.38
  255.2 1.8 fusion.38
  263.7 1.8 fusion.38
  272.2 1.8 fusion.38
  280.7 1.8 fusion.38
  289.2 1.8 fusion.38
  306.3 1.8 fusion.38
  314.8 1.8 fusion.38
  331.8 1.8 fusion.38
  340.4 1.8 fusion.38
  357.4 1.8 fusion.38
  365.9 1.8 fusion.38
  383.0 1.8 fusion.38
  391.5 1.8 fusion.38
  (378 shorter events, 208.2 us)
Async XLA Ops:
  7.2 116.0 %copy-start = (s32[32]{0:T(128)S(1)}, s32[32]{0:T(128)}, u32[]{:S(2)}) copy-start(s32[32]{0:T(128)} %param.10) | copy-start | bytes 388
  7.2 116.0 %all-gather.2.cloned.1.call-start = ((), (), s32[]{:S(2)}) async-start(), calls=%async_computation.2 | async-start | bytes 10813440 | tf_op jit(solution)/shard_map/all_gather | solution.py:57
  22.9 9.4 %all-to-all-start.1 = ((bf16[4,2,16,2,2,128]{5,4,3,2,1,0:T(2,128)(2,1)}), bf16[4,2,16,2,2,128]{5,4,3,2,1,0:T(2,128)(2,1)S(1)}, u32[]{:S(2)}, u32[]{:S(2)}) async-start(bf16[4,2,16,2,2,128]{5,4,3,2,1,0:T(2,128)(2,1)} %bitcast.58), calls=%async_computation.1 | async-start | bytes 262144 | tf_op jit(solution)/shard_map/all_to_all | solution.py:104
Sparse Core Ops, SparseCore 0:
  10.6 112.5 all-gather.1
where the time goes:
time: 407 us; the launch traced here: 404 us
  matrix products  100 us (25%)
  other arithmetic  98.6 us (24%)
  waiting for transfers between devices  94.2 us (23%)
  local copies, waits for them, and re-layouts  57.4 us (14%)
  loops' own time  24.1 us (6%)
  between operations  14.1 us (3%)
  blocking collectives  9.47 us (2%)
  starting transfers between devices  5.46 us (1%)
    all_gather x1, waiting for transfers between devices, attention(): arrived_rows = lax.all_gather(local_kv, 'ctx', axis=0, tiled=True)  90.2 us
    dot_general x32, matrix products, attend(): jnp.einsum('qd,kd->qk', query_mat, key_rows, preferred_element_type=jnp.f...  57 us
    dot_general x32, matrix products, attend(): jnp.dot(weights.astype(jnp.bfloat16), value_rows, preferred_element_type=...  43.1 us
    reduce_sum x32, other arithmetic, shard_length(): jnp.sum(jnp.where(jnp.arange(cache_lengths.shape[0]) == shard_id, cache_l...  40.7 us
    reduce_sum x32, other arithmetic, attend(): running_sum = running_sum * factor + jnp.sum(weights, axis=1)  36.3 us
    squeeze x32, local copies, waits for them, and re-layouts, attention(): lax.scan(visit, empty_state, (stacked, jnp.arange(shard_count, dtype=jnp....  32.2 us
    another operation x1, loops' own time, attention(): lax.scan(visit, empty_state, (stacked, jnp.arange(shard_count, dtype=jnp....  24.1 us
    dynamic_slice x32, local copies, waits for them, and re-layouts, attention(): lax.scan(visit, empty_state, (stacked, jnp.arange(shard_count, dtype=jnp....  20.7 us
  transfers between devices with their start and end apart: 2, of which 2 were waited for; matrix products, arithmetic and copies ran while one was open for 1% of the time, Pallas kernels for 0%

commit v1 on v0

v1 whole, which is shorter than its diff:
```python
import functools
import math

import jax
import jax.numpy as jnp
from jax import lax
from jax.experimental import pallas as pl
from jax.experimental.pallas import tpu as pltpu
from jax.sharding import PartitionSpec as P

MESH = pl.DeviceIdType.MESH
NY, NZ = 4, 8
NH, NI = 2, 4
HD = 128
GROUP = 8
TOK = 128
ROWS = TOK * GROUP
CACHE = 512
HALF = CACHE // 2
STEP = 4 * HALF
PAIR = 2 * TOK
TILE = 512
NQT = NY * ROWS // TILE
BLOCK = 16
PAGES = TOK // BLOCK
CAP = PAGES // 2
SCALE = HD ** -0.5 * math.log2(math.e)
LOWEST = -1.0e30
NT = (((1,), (1,)), ((), ()))

HALVES = (
    (0, 0), (0, 1), (1, 0), (-1, 0),
    (1, 1), (-1, 1), (2, 0), (-2, 0),
    (2, 1), (-2, 1), (3, 0), (-3, 0),
    (3, 1), (-3, 1), (4, 0), (4, 1),
)
TO_NEXT = {0: 3, 1: 5, 3: 7, 5: 9, 7: 11, 9: 13, 11: 14}
TO_PREV = {0: 2, 1: 4, 2: 6, 4: 8, 6: 10, 8: 12, 12: 15}
OFFSETS = (0, 1, 3, 2)


def kernel(lens, plan, q_in, cache_in, fresh_in, out, moved,
           kv, st, qs, acc, top, sbuf, wide, packed, osend, lsend, oget, lget,
           kv_s, kv_r, st_s, st_r, sh_s, sh_r, q_s, q_r, o_s, o_r, l_s, l_r, mg_s, mg_r, own_s):
    ctx = lax.axis_index("ctx")
    head = lax.axis_index("head")
    inst = lax.axis_index("inst")
    y, z = ctx // NZ, ctx % NZ
    me = head * NI + inst

    def at_z(d):
        return (y * NZ + (z + d + NZ) % NZ, head, inst)

    def at_y(d):
        return (((y + d + NY) % NY) * NZ + z, head, inst)

    def at_head(h):
        return (ctx, h // NI, h % NI)

    barrier = pltpu.get_barrier_semaphore()
    peers = [at_z(1), at_z(-1), at_y(1), at_y(2), at_y(3)]
    peers += [at_head((me + d) % (NH * NI)) for d in range(1, NH * NI)]
    for peer in peers:
        pl.semaphore_signal(barrier, inc=1, device_id=peer, device_id_type=MESH)

    length = lens[ctx]
    wide[...] = cache_in[...].astype(jnp.float32)
    slot_no = lax.broadcasted_iota(jnp.int32, (CACHE, HD), 0)
    keys = wide[pl.ds(0, CACHE, stride=2), :]
    values = wide[pl.ds(1, CACHE, stride=2), :]
    keys = jnp.where(slot_no < length, keys, jnp.broadcast_to(keys[0:1, :], (CACHE, HD)))
    values = jnp.where(slot_no < length, values, 0.0)
    kv[pl.ds(0, CACHE), 0:HD] = keys.astype(jnp.bfloat16)
    kv[pl.ds(0, CACHE), HD:2 * HD] = values.astype(jnp.bfloat16)
    fresh = fresh_in[...].astype(jnp.float32)
    wide[pl.ds(0, 2 * TOK), :] = fresh
    mine = st.at[pl.ds(NZ * TOK, TOK)]
    mine[:, 0:HD] = wide[pl.ds(0, TOK, stride=2), :].astype(jnp.bfloat16)
    mine[:, HD:2 * HD] = wide[pl.ds(1, TOK, stride=2), :].astype(jnp.bfloat16)
    qs[pl.ds(0, ROWS), :] = q_in[...]

    def kv_copy(src, forward):
        dst = (TO_NEXT if forward else TO_PREV)[src]
        return pltpu.make_async_remote_copy(
            src_ref=kv.at[pl.ds(src * HALF, HALF), pl.ds(0, 2 * HD)],
            dst_ref=kv.at[pl.ds(dst * HALF, HALF), pl.ds(0, 2 * HD)],
            send_sem=kv_s.at[dst],
            recv_sem=kv_r.at[dst],
            device_id=at_z(1 if forward else -1),
            device_id_type=MESH,
        )

    def kv_arrived(dst):
        forward = dst in TO_NEXT.values()
        src = {b: a for a, b in (TO_NEXT if forward else TO_PREV).items()}[dst]
        kv_copy(src, forward).wait_recv()

    def kv_sent(dst):
        forward = dst in TO_NEXT.values()
        src = {b: a for a, b in (TO_NEXT if forward else TO_PREV).items()}[dst]
        kv_copy(src, forward).wait_send()

    def q_copy(n):
        half = (0, 1, 0, 1, 0, 1)[n]
        src = (0, 0, 0, 0, 2, 1)[n]
        dst = (2, 2, 1, 1, 3, 3)[n]
        to = (1, 1, -1, -1, 1, -1)[n]
        return pltpu.make_async_remote_copy(
            src_ref=qs.at[pl.ds(src * ROWS + half * TILE, TILE)],
            dst_ref=qs.at[pl.ds(dst * ROWS + half * TILE, TILE)],
            send_sem=q_s.at[n],
            recv_sem=q_r.at[n],
            device_id=at_y(to),
            device_id_type=MESH,
        )

    def place(zz):
        return ((zz % NY) * 2 + zz // NY) * TOK

    def shift_copy():
        return pltpu.make_async_remote_copy(
            src_ref=st.at[pl.ds(NZ * TOK, TOK), pl.ds(0, 2 * HD)],
            dst_ref=st.at[pl.ds(pl.multiple_of(place(z), TOK), TOK), pl.ds(0, 2 * HD)],
            send_sem=sh_s,
            recv_sem=sh_r,
            device_id=(((y - z + NZ) % NY) * NZ + z, head, inst),
            device_id_type=MESH,
        )

    def stay_copy():
        return pltpu.make_async_copy(
            st.at[pl.ds(NZ * TOK, TOK), pl.ds(0, 2 * HD)],
            st.at[pl.ds(pl.multiple_of(place(z), TOK), TOK), pl.ds(0, 2 * HD)],
            sh_r,
        )

    def st_rows(zz, hop, forward):
        start = place((zz + NZ) % NZ)
        if hop < 4:
            return pl.ds(pl.multiple_of(start, TOK), TOK)
        half = TOK // 2
        return pl.ds(pl.multiple_of(start + (0 if forward else half), half), half)

    def st_copy(hop, forward):
        sign = 1 if forward else -1
        rows = st_rows(z - sign * (hop - 1), hop, forward)
        return pltpu.make_async_remote_copy(
            src_ref=st.at[rows, pl.ds(0, 2 * HD)],
            dst_ref=st.at[rows, pl.ds(0, 2 * HD)],
            send_sem=st_s.at[hop - 1, int(forward)],
            recv_sem=st_r.at[hop - 1, int(forward)],
            device_id=at_z(sign),
            device_id_type=MESH,
        )

    def st_arrived(hop, forward):
        sign = 1 if forward else -1
        rows = st_rows(z - sign * hop, hop, forward)
        pltpu.make_async_remote_copy(
            src_ref=st.at[rows, pl.ds(0, 2 * HD)],
            dst_ref=st.at[rows, pl.ds(0, 2 * HD)],
            send_sem=st_s.at[hop - 1, int(forward)],
            recv_sem=st_r.at[hop - 1, int(forward)],
            device_id=at_z(sign),
            device_id_type=MESH,
        ).wait_recv()

    def page_copy(d, dst):
        to = (me + d) % (NH * NI)
        return pltpu.make_async_remote_copy(
            src_ref=packed.at[(to % NI) * NH + to // NI],
            dst_ref=moved.at[dst],
            send_sem=mg_s.at[d],
            recv_sem=mg_r.at[d],
            device_id=at_head(to),
            device_id_type=MESH,
        )

    def own_pages():
        return pltpu.make_async_copy(packed.at[inst * NH + head], moved.at[me], own_s)

    def o_copy(a):
        return pltpu.make_async_remote_copy(
            src_ref=osend.at[a - 1],
            dst_ref=oget.at[a - 1],
            send_sem=o_s.at[a - 1],
            recv_sem=o_r.at[a - 1],
            device_id=at_y(OFFSETS[a]),
            device_id_type=MESH,
        )

    def l_copy(a):
        return pltpu.make_async_remote_copy(
            src_ref=lsend.at[a - 1],
            dst_ref=lget.at[a - 1],
            send_sem=l_s.at[a - 1],
            recv_sem=l_r.at[a - 1],
            device_id=at_y(OFFSETS[a]),
            device_id_type=MESH,
        )

    pl.semaphore_wait(barrier, len(peers))

    for half in (0, 1):
        kv_copy(half, True).start()
        kv_copy(half, False).start()
        q_copy(half).start()
        q_copy(2 + half).start()

    @pl.when(z % NY != 0)
    def _():
        shift_copy().start()

    @pl.when(z % NY == 0)
    def _():
        stay_copy().start()

    targets = []
    for b in range(PAGES):
        earlier = jnp.int32(0)
        for a in range(b):
            earlier = earlier + (plan[a] == plan[b]).astype(jnp.int32)
        targets.append(plan[b] * CAP + earlier)
    for t in range(NI * CAP):
        page = jnp.zeros((2 * BLOCK, HD), jnp.float32)
        for b in range(PAGES):
            page = page + fresh[2 * BLOCK * b:2 * BLOCK * (b + 1), :] * (targets[b] == t).astype(jnp.float32)
        packed[t // 2, pl.ds((t % 2) * 2 * BLOCK, 2 * BLOCK), :] = page.astype(jnp.bfloat16)
    for d in range(1, NH * NI):
        page_copy(d, me).start()
    own_pages().start()

    row_no = lax.broadcasted_iota(jnp.int32, (HALF, HD), 0)
    for n, (d, half) in enumerate(HALVES):
        filled = lens[y * NZ + (z + d + NZ) % NZ]
        kv[pl.ds(n * HALF, HALF), 2 * HD:3 * HD] = jnp.where(
            row_no + half * HALF < filled, 1.0, 0.0
        ).astype(jnp.bfloat16)
    st[pl.ds(0, NZ * TOK), 2 * HD:3 * HD] = jnp.ones((NZ * TOK, HD), jnp.bfloat16)

    def empty(n, carry):
        rows = pl.ds(pl.multiple_of(n * TILE, TILE), TILE)
        acc[rows, :] = jnp.zeros((TILE, 2 * HD), jnp.float32)
        top[rows, :] = jnp.full((TILE, HD), LOWEST, jnp.float32)
        return carry

    lax.fori_loop(0, NQT, empty, 0)

    def add(rows, scores, vals):
        before = top[rows, :]
        peak = jnp.maximum(before, jnp.max(scores, axis=1, keepdims=True) * SCALE)
        factor = jnp.exp2(before - peak)
        weights = jnp.exp2(scores * SCALE - peak[:, :1]).astype(jnp.bfloat16)
        part = jnp.dot(weights, vals, preferred_element_type=jnp.float32)
        acc[rows, :] = acc[rows, :] * jnp.concatenate([factor, factor], axis=1) + part
        top[rows, :] = peak

    def q_rows(i):
        return pl.ds(pl.multiple_of((i % NQT) * TILE, TILE), TILE)

    def kv_rows(i):
        return pl.ds(pl.multiple_of((i // NQT) * STEP, STEP), STEP)

    def score(i, slot):
        sbuf[slot] = lax.dot_general(
            qs[q_rows(i), :], kv[kv_rows(i), 0:HD], NT, preferred_element_type=jnp.float32
        )

    def weigh(i, slot):
        add(q_rows(i), sbuf[slot], kv[kv_rows(i), HD:3 * HD])

    def pass_on(dst):
        kv_arrived(dst)
        if dst in TO_NEXT and dst not in TO_PREV:
            kv_copy(dst, True).start()
        elif dst in TO_PREV:
            kv_copy(dst, False).start()

    def at_0():
        q_copy(2).wait_recv()

    def at_1():
        q_copy(3).wait_recv()
        q_copy(5).start()
        q_copy(0).wait_recv()
        q_copy(4).start()
        pass_on(4)
        pass_on(5)

    def at_2():
        q_copy(1).wait_recv()
        q_copy(4).wait_recv()

        @pl.when(z % NY != 0)
        def _():
            shift_copy().wait_recv()

        @pl.when(z % NY == 0)
        def _():
            stay_copy().wait()

        for forward in (True, False):
            st_copy(1, forward).start()

    def at_3():
        q_copy(5).wait_recv()
        pass_on(6)
        pass_on(7)

    def at_4():
        pass_on(8)
        pass_on(9)

    def next_stretch(hop):
        for forward in (True, False):
            st_arrived(hop, forward)
            st_copy(hop + 1, forward).start()

    def at_6():
        pass_on(10)
        pass_on(11)

    def at_8():
        pass_on(12)
        pass_on(13)

    def at_11():
        pass_on(14)
        pass_on(15)

    events = {
        0: at_0, 1: at_1, 2: at_2, 3: at_3, 4: at_4, 5: lambda: next_stretch(1), 6: at_6,
        7: lambda: next_stretch(2), 8: at_8, 9: lambda: next_stretch(3), 11: at_11,
    }

    pass_on(2)
    pass_on(3)
    score(0, 0)
    last = 4 * NQT // 2 - 1

    def two_tiles(n, carry):
        for when, event in events.items():
            pl.when(n == when)(event)
        for u in (0, 1):
            i = 2 * n + u
            score(i + 1, 1 - u)
            weigh(i, u)
        return carry

    lax.fori_loop(0, last, two_tiles, 0)
    score(2 * last + 1, 1)
    weigh(2 * last, 0)
    weigh(2 * last + 1, 1)

    for forward in (True, False):
        st_arrived(4, forward)

    eye = (
        lax.broadcasted_iota(jnp.int32, (HD, HD), 0) == lax.broadcasted_iota(jnp.int32, (HD, HD), 1)
    ).astype(jnp.float32)

    def stretch(a, row):
        starts = [pl.multiple_of(((j - y + NY) % NY) * PAIR, PAIR) for j in range(row + 1)]
        k_here = jnp.concatenate([st[pl.ds(s, PAIR), 0:HD] for s in starts], axis=0)
        v_here = jnp.concatenate([st[pl.ds(s, PAIR), HD:3 * HD] for s in starts], axis=0)
        column = lax.broadcasted_iota(jnp.int32, (TILE, PAIR), 1)
        token = lax.broadcasted_iota(jnp.int32, (TILE, PAIR), 0) // GROUP
        first = ((row - y + NY) % NY) * TOK
        key_pos = first + column + jnp.where(column >= TOK, NY * TOK - TOK, 0)
        tiles = [pl.ds(pl.multiple_of(a * ROWS + n * TILE, TILE), TILE) for n in range(ROWS // TILE)]
        scored = []
        for n, rows in enumerate(tiles):
            s = lax.dot_general(qs[rows, :], k_here, NT, preferred_element_type=jnp.float32)
            usable = key_pos <= z * TOK + n * (TILE // GROUP) + token
            own = jnp.where(usable, s[:, row * PAIR:], LOWEST)
            scored.append(own if row == 0 else jnp.concatenate([s[:, :row * PAIR], own], axis=1))
        for rows, s in zip(tiles, scored):
            add(rows, s, v_here)

    def finish(rows):
        part = acc[rows, :]
        total = part[:, HD:]
        result = part[:, :HD] / total
        level = top[rows, :] + jnp.log2(total)
        return result, level

    def stretch_of(a):
        offset = jnp.where(a == 0, 0, jnp.where(a == 1, 1, jnp.where(a == 2, 3, 2)))
        mine_row = (y + offset) % NY
        for row in range(NY):
            pl.when(mine_row == row)(functools.partial(stretch, a, row))

    def hand_back(a):
        stretch_of(a)
        for n in range(ROWS // HD):
            result, level = finish(pl.ds(pl.multiple_of(a * ROWS + n * HD, HD), HD))
            osend[a - 1, pl.ds(n * HD, HD), :] = result.astype(jnp.bfloat16)
            lsend[a - 1, pl.ds(n, 1), :] = jnp.sum(level * eye, axis=0, keepdims=True)

    for a in (3, 1, 2):
        hand_back(a)
        o_copy(a).start()
        l_copy(a).start()
    stretch_of(0)

    levels = []
    for n in range(ROWS // HD):
        result, level = finish(pl.ds(n * HD, HD))
        acc[pl.ds(n * HD, HD), 0:HD] = result
        levels.append(jnp.sum(level * eye, axis=0, keepdims=True))
    levels = [jnp.concatenate(levels, axis=0)]
    for a in (3, 1, 2):
        l_copy(a).wait_recv()
        levels.append(lget[a - 1])
    peak = functools.reduce(jnp.maximum, levels)
    shares = [jnp.exp2(level - peak) for level in levels]
    total = functools.reduce(jnp.add, shares)
    shares = [share / total for share in shares]
    for a in (3, 1, 2):
        o_copy(a).wait_recv()
    ones = jnp.ones((2 * HD, HD), jnp.bfloat16)
    for n in range(ROWS // HD):
        rows = pl.ds(n * HD, HD)
        result = jnp.zeros((HD, HD), jnp.float32)
        for share, part in zip(shares, (acc[rows, 0:HD], oget[2, rows, :], oget[0, rows, :], oget[1, rows, :])):
            diagonal = jnp.broadcast_to(share[n:n + 1, :], (HD, HD)) * eye
            high = diagonal.astype(jnp.bfloat16)
            low = (diagonal - high.astype(jnp.float32)).astype(jnp.bfloat16)
            spread = jnp.dot(jnp.concatenate([high, low], axis=1), ones, preferred_element_type=jnp.float32)
            result = result + spread * part.astype(jnp.float32)
        out[rows, :] = result.astype(jnp.bfloat16)

    for dst in range(2, 16):
        kv_sent(dst)
    for n in range(6):
        q_copy(n).wait_send()
    for hop in (1, 2, 3, 4):
        for forward in (True, False):
            st_copy(hop, forward).wait_send()

    @pl.when(z % NY != 0)
    def _():
        shift_copy().wait_send()

    for a in (1, 2, 3):
        o_copy(a).wait_send()
        l_copy(a).wait_send()
    for d in range(1, NH * NI):
        page_copy(d, me).wait_send()
        page_copy(d, (me - d + NH * NI) % (NH * NI)).wait_recv()
    own_pages().wait()


def body(queries, cache_kv, new_kv, cache_lengths, plan):
    smem = pl.BlockSpec(memory_space=pltpu.SMEM)
    vmem = pl.BlockSpec(memory_space=pltpu.VMEM)
    heads = NH * NI
    out, moved = pl.pallas_call(
        kernel,
        out_shape=(
            jax.ShapeDtypeStruct((ROWS, HD), jnp.bfloat16),
            jax.ShapeDtypeStruct((heads, 4 * BLOCK, HD), jnp.bfloat16),
        ),
        in_specs=[smem, smem, vmem, vmem, vmem],
        out_specs=(vmem, pl.BlockSpec(memory_space=pl.ANY)),
        scratch_shapes=[
            pltpu.VMEM((16 * HALF, 3 * HD), jnp.bfloat16),
            pltpu.VMEM(((NZ + 1) * TOK, 3 * HD), jnp.bfloat16),
            pltpu.VMEM((NY * ROWS, HD), jnp.bfloat16),
            pltpu.VMEM((NY * ROWS, 2 * HD), jnp.float32),
            pltpu.VMEM((NY * ROWS, HD), jnp.float32),
            pltpu.VMEM((2, TILE, STEP), jnp.float32),
            pltpu.VMEM((2 * CACHE, HD), jnp.float32),
            pltpu.VMEM((heads, 4 * BLOCK, HD), jnp.bfloat16),
            pltpu.VMEM((3, ROWS, HD), jnp.bfloat16),
            pltpu.VMEM((3, ROWS // HD, HD), jnp.float32),
            pltpu.VMEM((3, ROWS, HD), jnp.bfloat16),
            pltpu.VMEM((3, ROWS // HD, HD), jnp.float32),
            pltpu.SemaphoreType.DMA((16,)),
            pltpu.SemaphoreType.DMA((16,)),
            pltpu.SemaphoreType.DMA((4, 2)),
            pltpu.SemaphoreType.DMA((4, 2)),
            pltpu.SemaphoreType.DMA,
            pltpu.SemaphoreType.DMA,
            pltpu.SemaphoreType.DMA((6,)),
            pltpu.SemaphoreType.DMA((6,)),
            pltpu.SemaphoreType.DMA((3,)),
            pltpu.SemaphoreType.DMA((3,)),
            pltpu.SemaphoreType.DMA((3,)),
            pltpu.SemaphoreType.DMA((3,)),
            pltpu.SemaphoreType.DMA((heads,)),
            pltpu.SemaphoreType.DMA((heads,)),
            pltpu.SemaphoreType.DMA,
        ],
        compiler_params=pltpu.CompilerParams(
            collective_id=0, has_side_effects=True, vmem_limit_bytes=48 * 2 ** 20
        ),
        name="stretch_attention",
    )(
        cache_lengths,
        plan.reshape(PAGES),
        queries.reshape(ROWS, HD),
        cache_kv.reshape(2 * CACHE, HD),
        new_kv.reshape(2 * TOK, HD),
    )
    attended = out.reshape(TOK, 1, GROUP, HD)
    moved = moved.reshape(heads, 2, BLOCK, 2, HD)
    migrated = jnp.transpose(moved, (1, 2, 3, 0, 4)).reshape(1, 1, 2, BLOCK, 2, heads, HD)
    return attended, migrated


def solution(mesh):
    return jax.shard_map(
        body,
        mesh=mesh,
        in_specs=(
            P("ctx", ("head", "inst"), None, None),
            P("ctx", None, ("head", "inst"), None),
            P("ctx", None, ("head", "inst"), None),
            P(),
            P("ctx", None),
        ),
        out_specs=(
            P("ctx", ("head", "inst"), None, None),
            P("inst", "ctx", "head", None, None, None, None),
        ),
        check_vma=False,
    )
```

time: 407 us -> 71.2 us (0.17)
  matrix products: 100 us -> 0 us
  other arithmetic: 98.6 us -> 0 us
  waiting for transfers between devices: 94.2 us -> 0 us
  Pallas kernels: 0 us -> 65.5 us
  local copies, waits for them, and re-layouts: 57.4 us -> 4.91 us
  loops' own time: 24.1 us -> 0 us
  between operations: 14.1 us -> 0.66 us
  blocking collectives: 9.47 us -> 0 us
  starting transfers between devices: 5.46 us -> 0 us
    dot_general x65 -> x0, matrix products: 100 us -> none  [the longest x32 57 us: attend(): jnp.einsum('qd,kd->qk', query_mat, key_rows, preferred_element_type=jnp.f...]
    all_gather x1 -> x0, waiting for transfers between devices: 90.2 us -> none  [attention(): arrived_rows = lax.all_gather(local_kv, 'ctx', axis=0, tiled=True)]
    reduce_sum x65 -> x0, other arithmetic: 77.7 us -> none  [the longest x32 40.7 us: shard_length(): jnp.sum(jnp.where(jnp.arange(cache_lengths.shape[0]) == shard_id, cache_l...]
    pallas_call x0 -> x1, Pallas kernels: none -> 65.5 us  [body(): pl.pallas_call(kernel, out_shape=(jax.ShapeDtypeStruct((ROWS, HD), jnp.bf...]
    squeeze x32 -> x0, local copies, waits for them, and re-layouts: 32.2 us -> none  [attention(): lax.scan(visit, empty_state, (stacked, jnp.arange(shard_count, dtype=jnp....]
    another operation x1 -> x0, loops' own time: 24.1 us -> none  [attention(): lax.scan(visit, empty_state, (stacked, jnp.arange(shard_count, dtype=jnp....]
    dynamic_slice x32 -> x0, local copies, waits for them, and re-layouts: 20.7 us -> none  [attention(): lax.scan(visit, empty_state, (stacked, jnp.arange(shard_count, dtype=jnp....]
    lt x32 -> x0, other arithmetic: 17.6 us -> none  [attend(): positions < length]
  transfers between devices with their start and end apart: 2 -> 0, of which waited for: 2 -> 0; matrix products, arithmetic and copies ran while one was open for 1% -> 0% of each run, Pallas kernels for 0% -> 0%
where the time goes in v1:
time: 71.2 us; the launch traced here: 71 us
  Pallas kernels  65.5 us (92%)
  local copies, waits for them, and re-layouts  4.91 us (7%)
    pallas_call x1, Pallas kernels, body(): pl.pallas_call(kernel, out_shape=(jax.ShapeDtypeStruct((ROWS, HD), jnp.bf...  65.5 us
    unnamed x11, local copies, waits for them, and re-layouts  4.1 us

profile of v1, /device:TPU:1, one launch (start us, length us, event | category | flops | bytes accessed | tf_op | source)
XLA Modules:
  0.0 71.0 jit_solution(17989085513717000707)
XLA Ops:
  0.6 0.0 copy-start.3
  0.6 0.0 copy-start.4
  0.7 0.6 copy-done.3
  1.3 0.0 copy-done.4
  1.3 0.0 copy-start
  1.3 0.9 %copy-done = bf16[128,1,8,128]{3,2,1,0:T(8,128)(2,1)S(1)} copy-done((bf16[128,1,8,128]{3,2,1,0:T(8,128)(2,1)S(1)}, bf16[128,1,8,128]{3,2,1,0:T(8,128)(2,1)}, u32[]{:S(2)}) %copy-start) | copy-done | bytes 262168
  2.3 0.0 copy-start.1
  2.3 0.9 %copy-done.1 = bf16[512,2,1,128]{3,1,2,0:T(2,128)(2,1)S(1)} copy-done((bf16[512,2,1,128]{3,1,2,0:T(2,128)(2,1)S(1)}, bf16[512,2,1,128]{3,1,2,0:T(2,128)(2,1)}, u32[]{:S(2)}) %copy-start.1) | copy-done | bytes 262168
  3.2 0.0 copy-start.2
  3.2 0.8 %copy-done.2 = bf16[128,2,1,128]{3,1,2,0:T(2,128)(2,1)S(1)} copy-done((bf16[128,2,1,128]{3,1,2,0:T(2,128)(2,1)S(1)}, bf16[128,2,1,128]{3,1,2,0:T(2,128)(2,1)}, u32[]{:S(2)}) %copy-start.2) | copy-done | bytes 65560
  4.0 65.5 %stretch_attention.1 = (bf16[1024,128]{1,0:T(8,128)(2,1)S(1)}, bf16[8,64,128]{2,1,0:T(8,128)(2,1)S(1)}) custom-call(s32[32]{0:T(128)S(1)} %copy-done.3, s32[8]{0:T(128)S(1)} %bitcast.18, bf16[1024,128]{1,0:T(8,128)(2,1)S(1)} %bitcast.13, bf16[1024,128]{1,0:T(8,128)(2,1)S(1)} %bitcast.14, bf16[256,128]{1,0:T(8,128)(2,1)S(1)} %bitcast.17), custom_call_target="tpu_custom_call" | custom-call | tf_op jit(solution)/shard_map/stretch_attention/pallas_call | solution.py:458
  69.5 0.8 %copy.10 = bf16[8,2,16,2,128]{4,0,3,2,1:T(8,128)(2,1)} copy(bf16[8,2,16,2,128]{4,3,2,1,0:T(2,128)(2,1)S(1)} %bitcast.16) | data formatting | bytes 262144 | tf_op jit(solution)/shard_map/reshape | solution.py:507
  70.3 0.7 copy.12
Async XLA Ops:
  0.6 0.7 copy-start.3
  0.6 0.7 copy-start.4
  1.3 0.9 %copy-start = (bf16[128,1,8,128]{3,2,1,0:T(8,128)(2,1)S(1)}, bf16[128,1,8,128]{3,2,1,0:T(8,128)(2,1)}, u32[]{:S(2)}) copy-start(bf16[128,1,8,128]{3,2,1,0:T(8,128)(2,1)} %param.5) | copy-start | bytes 786436
  2.3 0.9 %copy-start.1 = (bf16[512,2,1,128]{3,1,2,0:T(2,128)(2,1)S(1)}, bf16[512,2,1,128]{3,1,2,0:T(2,128)(2,1)}, u32[]{:S(2)}) copy-start(bf16[512,2,1,128]{3,1,2,0:T(2,128)(2,1)} %param.6) | copy-start | bytes 786436
  3.2 0.8 %copy-start.2 = (bf16[128,2,1,128]{3,1,2,0:T(2,128)(2,1)S(1)}, bf16[128,2,1,128]{3,1,2,0:T(2,128)(2,1)}, u32[]{:S(2)}) copy-start(bf16[128,2,1,128]{3,1,2,0:T(2,128)(2,1)} %param.7) | copy-start | bytes 196612

commit v2 on v0

v2 whole, which is shorter than its diff:
```python
import functools
import math

import jax
import jax.numpy as jnp
from jax import lax
from jax.experimental import pallas as pl
from jax.experimental.pallas import tpu as pltpu
from jax.sharding import PartitionSpec as P

MESH = pl.DeviceIdType.MESH
NY, NZ = 4, 8
NH, NI = 2, 4
HEADS = NH * NI
HD = 128
GROUP = 8
TOK = 128
ROWS = TOK * GROUP
CACHE = 512
PIECE = 128
OWN = CACHE // PIECE
MSGS = 14
PIECES = OWN + 2 * MSGS
PER_STEP = 8
STEP = PER_STEP * PIECE
TILE = 512
BLOCK = 16
PAGES = TOK // BLOCK
CAP = PAGES // 2
SUMS = 16
SCALE = HD ** -0.5 * math.log2(math.e)
LOWEST = -1.0e30
NT = (((1,), (1,)), ((), ()))
OFFSETS = (0, 1, 3, 2)


def piece_of(m, forward):
    return OWN + 2 * m + (0 if forward else 1)


def shard_of(m, forward):
    if m < 12:
        hop, quarter = 1 + m // OWN, m % OWN
    else:
        hop, quarter = 4, (m - 12 if forward else m - 10)
    return (-hop if forward else hop), quarter


def next_message(m, forward):
    if m < 8:
        return m + 4
    if forward and m in (8, 9):
        return m + 4
    if not forward and m in (10, 11):
        return m + 2
    return None


def kernel(lens, plan, q_in, cache_in, fresh_in, out, moved,
           kv, st, live, qs, acc, top, sbuf, raw, fraw, wide, packed, osend, lsend, oget, lget,
           in_s, kv_s, kv_r, st_s, st_r, sh_s, sh_r, q_s, q_r, o_s, o_r, l_s, l_r, mg_s, mg_r, own_s):
    ctx = lax.axis_index("ctx")
    head = lax.axis_index("head")
    inst = lax.axis_index("inst")
    y, z = ctx // NZ, ctx % NZ
    me = head * NI + inst

    def at_z(d):
        return (y * NZ + (z + d + NZ) % NZ, head, inst)

    def at_y(d):
        return (((y + d + NY) % NY) * NZ + z, head, inst)

    def at_head(h):
        return (ctx, h // NI, h % NI)

    loads = [
        pltpu.make_async_copy(cache_in.at[pl.ds(n * 2 * PIECE, 2 * PIECE)], raw.at[n], in_s.at[n])
        for n in range(OWN)
    ]
    loads.append(pltpu.make_async_copy(fresh_in, fraw, in_s.at[OWN]))
    loads.append(pltpu.make_async_copy(q_in, qs.at[pl.ds(0, ROWS)], in_s.at[OWN + 1]))
    for load in loads:
        load.start()

    barrier = pltpu.get_barrier_semaphore()
    peers = [at_z(1), at_z(-1), at_y(1), at_y(2), at_y(3)]
    peers += [at_head((me + d) % HEADS) for d in range(1, HEADS)]
    for peer in peers:
        pl.semaphore_signal(barrier, inc=1, device_id=peer, device_id_type=MESH)

    def kv_copy(m, forward):
        if m < OWN:
            src = m
        else:
            before = [b for b in range(MSGS) if next_message(b, forward) == m]
            src = piece_of(before[0], forward)
        dst = piece_of(m, forward)
        return pltpu.make_async_remote_copy(
            src_ref=kv.at[src],
            dst_ref=kv.at[dst],
            send_sem=kv_s.at[dst],
            recv_sem=kv_r.at[dst],
            device_id=at_z(1 if forward else -1),
            device_id_type=MESH,
        )

    def pass_on(m):
        for forward in (True, False):
            kv_copy(m, forward).wait_recv()
            later = next_message(m, forward)
            if later is not None:
                kv_copy(later, forward).start()

    def q_copy(n):
        half = (0, 1, 0, 1, 0, 1)[n]
        src = (0, 0, 0, 0, 2, 1)[n]
        dst = (2, 2, 1, 1, 3, 3)[n]
        to = (1, 1, -1, -1, 1, -1)[n]
        if n < 4:
            src_ref = q_in.at[pl.ds(half * TILE, TILE)]
        else:
            src_ref = qs.at[pl.ds(src * ROWS + half * TILE, TILE)]
        return pltpu.make_async_remote_copy(
            src_ref=src_ref,
            dst_ref=qs.at[pl.ds(dst * ROWS + half * TILE, TILE)],
            send_sem=q_s.at[n],
            recv_sem=q_r.at[n],
            device_id=at_y(to),
            device_id_type=MESH,
        )

    def place(zz):
        zz = (zz + NZ) % NZ
        return (zz % NY) * 2 + zz // NY

    def shift_copy():
        return pltpu.make_async_remote_copy(
            src_ref=st.at[NZ],
            dst_ref=st.at[place(z)],
            send_sem=sh_s,
            recv_sem=sh_r,
            device_id=(((y - z + NZ) % NY) * NZ + z, head, inst),
            device_id_type=MESH,
        )

    def stay_copy():
        return pltpu.make_async_copy(st.at[NZ], st.at[place(z)], sh_r)

    def st_ref(zz, hop, forward):
        if hop < 4:
            return st.at[place(zz)]
        return st.at[place(zz), pl.ds(0 if forward else TOK, TOK)]

    def st_copy(hop, forward, sending):
        sign = 1 if forward else -1
        ref = st_ref(z - sign * (hop - 1 if sending else hop), hop, forward)
        return pltpu.make_async_remote_copy(
            src_ref=ref,
            dst_ref=ref,
            send_sem=st_s.at[hop - 1, int(forward)],
            recv_sem=st_r.at[hop - 1, int(forward)],
            device_id=at_z(sign),
            device_id_type=MESH,
        )

    def next_stretch(hop):
        for forward in (True, False):
            st_copy(hop, forward, False).wait_recv()
            if hop < 4:
                st_copy(hop + 1, forward, True).start()

    def page_copy(d, dst):
        to = (me + d) % HEADS
        return pltpu.make_async_remote_copy(
            src_ref=packed.at[(to % NI) * NH + to // NI],
            dst_ref=moved.at[dst],
            send_sem=mg_s.at[d],
            recv_sem=mg_r.at[d],
            device_id=at_head(to),
            device_id_type=MESH,
        )

    def own_pages():
        return pltpu.make_async_copy(packed.at[inst * NH + head], moved.at[me], own_s)

    def o_copies(n):
        to = at_y((1, -1, 1, 1, -1, -1)[n])
        return (
            pltpu.make_async_remote_copy(
                src_ref=osend.at[n], dst_ref=oget.at[n], send_sem=o_s.at[n], recv_sem=o_r.at[n],
                device_id=to, device_id_type=MESH,
            ),
            pltpu.make_async_remote_copy(
                src_ref=lsend.at[n], dst_ref=lget.at[n], send_sem=l_s.at[n], recv_sem=l_r.at[n],
                device_id=to, device_id_type=MESH,
            ),
        )

    length = lens[ctx]

    def split(n):
        return wide[n, pl.ds(0, PIECE, stride=2), :], wide[n, pl.ds(1, PIECE, stride=2), :]

    def own_piece(n, first):
        loads[n].wait()
        wide[n] = raw[n].astype(jnp.float32)
        keys, values = split(n)
        first = keys[0:1, :] if n == 0 else first
        usable = lax.broadcasted_iota(jnp.int32, (PIECE, HD), 0) + n * PIECE < length
        kv[n, pl.ds(0, PIECE), :] = jnp.where(usable, keys, jnp.broadcast_to(first, (PIECE, HD))).astype(jnp.bfloat16)
        kv[n, pl.ds(PIECE, HD), :] = jnp.where(usable, values, 0.0).T.astype(jnp.bfloat16)
        return first

    first = own_piece(0, None)
    pl.semaphore_wait(barrier, len(peers))
    for forward in (True, False):
        kv_copy(0, forward).start()
    q_copy(0).start()
    q_copy(2).start()
    for n in range(1, OWN):
        own_piece(n, first)
        for forward in (True, False):
            kv_copy(n, forward).start()

    loads[OWN].wait()
    fresh = fraw[...].astype(jnp.float32)
    wide[OWN] = fresh
    keys, values = split(OWN)
    st[NZ, pl.ds(0, TOK), :] = keys.astype(jnp.bfloat16)
    st[NZ, pl.ds(TOK, HD), :] = values.T.astype(jnp.bfloat16)

    @pl.when(z % NY != 0)
    def _():
        shift_copy().start()

    @pl.when(z % NY == 0)
    def _():
        stay_copy().start()

    q_copy(1).start()
    q_copy(3).start()

    def empty(n, carry):
        acc[:, pl.ds(pl.multiple_of(n * TILE, TILE), TILE)] = jnp.zeros((HD + SUMS, TILE), jnp.float32)
        return carry

    lax.fori_loop(0, NY * ROWS // TILE, empty, 0)
    top[...] = jnp.full((1, NY * ROWS), LOWEST, jnp.float32)
    origin = {n: (0, n) for n in range(OWN)}
    for m in range(MSGS):
        for forward in (True, False):
            origin[piece_of(m, forward)] = shard_of(m, forward)
    lane = lax.broadcasted_iota(jnp.int32, (SUMS, PIECE), 1)
    for n in range(PIECES):
        d, quarter = origin[n]
        filled = lens[y * NZ + (z + d + NZ) % NZ]
        live[:, pl.ds(n * PIECE, PIECE)] = jnp.where(lane + quarter * PIECE < filled, 1.0, 0.0).astype(jnp.bfloat16)

    targets = []
    for b in range(PAGES):
        earlier = jnp.int32(0)
        for a in range(b):
            earlier = earlier + (plan[a] == plan[b]).astype(jnp.int32)
        targets.append(plan[b] * CAP + earlier)
    for t in range(NI * CAP):
        page = jnp.zeros((2 * BLOCK, HD), jnp.float32)
        for b in range(PAGES):
            page = page + fresh[2 * BLOCK * b:2 * BLOCK * (b + 1), :] * (targets[b] == t).astype(jnp.float32)
        packed[t // 2, pl.ds((t % 2) * 2 * BLOCK, 2 * BLOCK), :] = page.astype(jnp.bfloat16)
    for d in range(1, HEADS):
        page_copy(d, me).start()
    own_pages().start()

    def columns(a, half):
        return pl.ds(pl.multiple_of(a * ROWS + half * TILE, TILE), TILE)

    def add(cols, scores, vals):
        before = top[:, cols]
        peak = jnp.maximum(before, jnp.max(scores, axis=0, keepdims=True) * SCALE)
        weights = jnp.exp2(scores * SCALE - peak).astype(jnp.bfloat16)
        part = jnp.dot(vals, weights, preferred_element_type=jnp.float32)
        acc[:, cols] = acc[:, cols] * jnp.exp2(before - peak) + part
        top[:, cols] = peak

    def score(a, half, step, slot):
        keys = kv[pl.ds(step * PER_STEP, PER_STEP), pl.ds(0, PIECE), :].reshape(STEP, HD)
        sbuf[slot] = lax.dot_general(keys, qs[columns(a, half), :], NT, preferred_element_type=jnp.float32)

    def weigh(a, half, step, slot):
        vals = jnp.concatenate([kv[step * PER_STEP + n, pl.ds(PIECE, HD), :] for n in range(PER_STEP)], axis=1)
        sums = live[:, pl.ds(pl.multiple_of(step * STEP, STEP), STEP)]
        add(columns(a, half), sbuf[slot], jnp.concatenate([vals, sums], axis=0))

    def turn(n):
        return jnp.where(n < 4, n, (n + 1) % 4), n // 4

    def event_0():
        q_copy(2).wait_recv()
        pass_on(2)

    def event_1():
        q_copy(3).wait_recv()
        q_copy(5).start()
        q_copy(0).wait_recv()
        q_copy(4).start()
        pass_on(3)

        @pl.when(z % NY != 0)
        def _():
            shift_copy().wait_recv()

        @pl.when(z % NY == 0)
        def _():
            stay_copy().wait()

        for forward in (True, False):
            st_copy(1, forward, True).start()

    def event_2():
        q_copy(1).wait_recv()
        q_copy(4).wait_recv()
        pass_on(4)

    def event_3():
        q_copy(5).wait_recv()
        pass_on(5)

    def event_4():
        next_stretch(1)
        pass_on(6)

    def event_5():
        pass_on(7)

    def event_6():
        pass_on(8)

    def event_7():
        next_stretch(2)
        pass_on(9)

    def event_8():
        pass_on(10)

    def event_9():
        pass_on(11)

    def event_10():
        next_stretch(3)

    events = (
        event_0, event_1, event_2, event_3, event_4, event_5, event_6, event_7, event_8, event_9, event_10,
    )
    pass_on(0)
    pass_on(1)
    loads[OWN + 1].wait()
    score(0, 0, 0, 0)
    last = 11

    def one_turn(n, carry):
        for when, event in enumerate(events):
            pl.when(n == when)(event)
        a, step = turn(n)
        after, step_after = turn(n + 1)
        score(a, 1, step, 1)
        weigh(a, 0, step, 0)
        score(after, 0, step_after, 0)
        weigh(a, 1, step, 1)
        return carry

    lax.fori_loop(0, last, one_turn, 0)
    a, step = turn(last)
    score(a, 1, step, 1)
    weigh(a, 0, step, 0)
    weigh(a, 1, step, 1)

    def stretch(a, row):
        pairs = [(j - y + NY) % NY for j in range(row + 1)]
        keys = jnp.concatenate([st[pl.ds(2 * k, 2), pl.ds(0, TOK), :].reshape(2 * TOK, HD) for k in pairs], axis=0)
        vals = jnp.concatenate([st[2 * k + n, pl.ds(TOK, HD), :] for k in pairs for n in (0, 1)], axis=1)
        vals = jnp.concatenate([vals, jnp.ones((SUMS, 2 * TOK * (row + 1)), jnp.bfloat16)], axis=0)
        key = lax.broadcasted_iota(jnp.int32, (2 * TOK, TILE), 0)
        token = lax.broadcasted_iota(jnp.int32, (2 * TOK, TILE), 1) // GROUP
        key_pos = pairs[row] * TOK + key + jnp.where(key >= TOK, NY * TOK - TOK, 0)
        scored = []
        for half in (0, 1):
            s = lax.dot_general(keys, qs[columns(a, half), :], NT, preferred_element_type=jnp.float32)
            usable = key_pos <= z * TOK + half * (TILE // GROUP) + token
            own = jnp.where(usable, s[row * 2 * TOK:, :], LOWEST)
            scored.append(own if row == 0 else jnp.concatenate([s[:row * 2 * TOK, :], own], axis=0))
        for half in (0, 1):
            add(columns(a, half), scored[half], vals)

    def stretch_of(a):
        offset = jnp.where(a == 3, 2, jnp.where(a == 2, 3, a))
        mine_row = (y + offset) % NY
        for row in range(NY):
            pl.when(mine_row == row)(functools.partial(stretch, a, row))

    next_stretch(4)

    def stretch_turn(n, carry):
        stretch_of(jnp.where(n == 0, 3, n))
        return carry

    lax.fori_loop(0, 3, stretch_turn, 0)

    def finish(a, half):
        cols = columns(a, half)
        part = acc[:, cols]
        total = part[HD:HD + 1, :]
        return part[:HD, :] * (1.0 / total), top[:, cols] + jnp.log2(total)

    def join(parts):
        peak = functools.reduce(jnp.maximum, [level for _, level in parts])
        shares = [jnp.exp2(level - peak) for _, level in parts]
        total = functools.reduce(jnp.add, shares)
        result = functools.reduce(
            jnp.add, [part.astype(jnp.float32) * (share / total) for (part, _), share in zip(parts, shares)]
        )
        return result, peak + jnp.log2(total)

    def arrived(n):
        for copy in o_copies(n):
            copy.wait_recv()
        return oget[n], lget[n]

    def send(n, result, level):
        osend[n] = result.astype(jnp.bfloat16)
        lsend[n] = level
        for copy in o_copies(n):
            copy.start()

    pass_on(12)
    pass_on(13)
    order = (3, 1, 2, 0)
    score(order[0], 0, 3, 0)
    for n, a in enumerate(order):
        score(a, 1, 3, 1)
        weigh(a, 0, 3, 0)
        if n < 3:
            score(order[n + 1], 0, 3, 0)
        weigh(a, 1, 3, 1)
        if a == 3:
            send(0, *finish(3, 0))
            send(1, *finish(3, 1))
        if a == 1:
            send(3, *finish(1, 1))
        if a == 2:
            send(4, *finish(2, 0))
            send(2, *join([finish(1, 0), arrived(0)]))
            send(5, *join([finish(2, 1), arrived(1)]))
    stretch_of(0)

    for half in (0, 1):
        result, _ = join([finish(0, half), arrived(2 + half), arrived(4 + half)])
        out[pl.ds(half * TILE, TILE), :] = result.T.astype(jnp.bfloat16)

    for m in range(MSGS):
        for forward in (True, False):
            kv_copy(m, forward).wait_send()
    for n in range(6):
        q_copy(n).wait_send()
    for hop in (1, 2, 3, 4):
        for forward in (True, False):
            st_copy(hop, forward, True).wait_send()

    @pl.when(z % NY != 0)
    def _():
        shift_copy().wait_send()

    for n in range(6):
        for copy in o_copies(n):
            copy.wait_send()
    for d in range(1, HEADS):
        page_copy(d, me).wait_send()
        page_copy(d, (me - d + HEADS) % HEADS).wait_recv()
    own_pages().wait()


def body(queries, cache_kv, new_kv, cache_lengths, plan):
    smem = pl.BlockSpec(memory_space=pltpu.SMEM)
    hbm = pl.BlockSpec(memory_space=pltpu.HBM)
    out, moved = pl.pallas_call(
        kernel,
        out_shape=(
            jax.ShapeDtypeStruct((ROWS, HD), jnp.bfloat16),
            jax.ShapeDtypeStruct((HEADS, 4 * BLOCK, HD), jnp.bfloat16),
        ),
        in_specs=[smem, smem, hbm, hbm, hbm],
        out_specs=(pl.BlockSpec(memory_space=pltpu.VMEM), pl.BlockSpec(memory_space=pl.ANY)),
        scratch_shapes=[
            pltpu.VMEM((PIECES, PIECE + HD, HD), jnp.bfloat16),
            pltpu.VMEM((NZ + 1, TOK + HD, HD), jnp.bfloat16),
            pltpu.VMEM((SUMS, PIECES * PIECE), jnp.bfloat16),
            pltpu.VMEM((NY * ROWS, HD), jnp.bfloat16),
            pltpu.VMEM((HD + SUMS, NY * ROWS), jnp.float32),
            pltpu.VMEM((1, NY * ROWS), jnp.float32),
            pltpu.VMEM((2, STEP, TILE), jnp.float32),
            pltpu.VMEM((OWN, 2 * PIECE, HD), jnp.bfloat16),
            pltpu.VMEM((2 * TOK, HD), jnp.bfloat16),
            pltpu.VMEM((OWN + 1, 2 * PIECE, HD), jnp.float32),
            pltpu.VMEM((HEADS, 4 * BLOCK, HD), jnp.bfloat16),
            pltpu.VMEM((6, HD, TILE), jnp.bfloat16),
            pltpu.VMEM((6, 1, TILE), jnp.float32),
            pltpu.VMEM((6, HD, TILE), jnp.bfloat16),
            pltpu.VMEM((6, 1, TILE), jnp.float32),
            pltpu.SemaphoreType.DMA((OWN + 2,)),
            pltpu.SemaphoreType.DMA((PIECES,)),
            pltpu.SemaphoreType.DMA((PIECES,)),
            pltpu.SemaphoreType.DMA((4, 2)),
            pltpu.SemaphoreType.DMA((4, 2)),
            pltpu.SemaphoreType.DMA,
            pltpu.SemaphoreType.DMA,
            pltpu.SemaphoreType.DMA((6,)),
            pltpu.SemaphoreType.DMA((6,)),
            pltpu.SemaphoreType.DMA((6,)),
            pltpu.SemaphoreType.DMA((6,)),
            pltpu.SemaphoreType.DMA((6,)),
            pltpu.SemaphoreType.DMA((6,)),
            pltpu.SemaphoreType.DMA((HEADS,)),
            pltpu.SemaphoreType.DMA((HEADS,)),
            pltpu.SemaphoreType.DMA,
        ],
        compiler_params=pltpu.CompilerParams(
            collective_id=0, has_side_effects=True, vmem_limit_bytes=58 * 2 ** 20
        ),
        name="stretch_attention",
    )(
        cache_lengths,
        plan.reshape(PAGES),
        queries.reshape(ROWS, HD),
        cache_kv.reshape(2 * CACHE, HD),
        new_kv.reshape(2 * TOK, HD),
    )
    attended = out.reshape(TOK, 1, GROUP, HD)
    moved = moved.reshape(HEADS, 2, BLOCK, 2, HD)
    migrated = jnp.transpose(moved, (1, 2, 3, 0, 4)).reshape(1, 1, 2, BLOCK, 2, HEADS, HD)
    return attended, migrated


def solution(mesh):
    return jax.shard_map(
        body,
        mesh=mesh,
        in_specs=(
            P("ctx", ("head", "inst"), None, None),
            P("ctx", None, ("head", "inst"), None),
            P("ctx", None, ("head", "inst"), None),
            P(),
            P("ctx", None),
        ),
        out_specs=(
            P("ctx", ("head", "inst"), None, None),
            P("inst", "ctx", "head", None, None, None, None),
        ),
        check_vma=False,
    )
```

time: 407 us -> 58.5 us (0.14)
  matrix products: 100 us -> 0 us
  other arithmetic: 98.6 us -> 0 us
  waiting for transfers between devices: 94.2 us -> 0 us
  local copies, waits for them, and re-layouts: 57.4 us -> 2.47 us
  Pallas kernels: 0 us -> 54.5 us
  loops' own time: 24.1 us -> 0 us
  between operations: 14.1 us -> 0.65 us
  blocking collectives: 9.47 us -> 0 us
  starting transfers between devices: 5.46 us -> 0 us
    dot_general x65 -> x0, matrix products: 100 us -> none  [the longest x32 57 us: attend(): jnp.einsum('qd,kd->qk', query_mat, key_rows, preferred_element_type=jnp.f...]
    all_gather x1 -> x0, waiting for transfers between devices: 90.2 us -> none  [attention(): arrived_rows = lax.all_gather(local_kv, 'ctx', axis=0, tiled=True)]
    reduce_sum x65 -> x0, other arithmetic: 77.7 us -> none  [the longest x32 40.7 us: shard_length(): jnp.sum(jnp.where(jnp.arange(cache_lengths.shape[0]) == shard_id, cache_l...]
    pallas_call x0 -> x1, Pallas kernels: none -> 54.5 us  [body(): pl.pallas_call(kernel, out_shape=(jax.ShapeDtypeStruct((ROWS, HD), jnp.bf...]
    squeeze x32 -> x0, local copies, waits for them, and re-layouts: 32.2 us -> none  [attention(): lax.scan(visit, empty_state, (stacked, jnp.arange(shard_count, dtype=jnp....]
    another operation x1 -> x0, loops' own time: 24.1 us -> none  [attention(): lax.scan(visit, empty_state, (stacked, jnp.arange(shard_count, dtype=jnp....]
    dynamic_slice x32 -> x0, local copies, waits for them, and re-layouts: 20.7 us -> none  [attention(): lax.scan(visit, empty_state, (stacked, jnp.arange(shard_count, dtype=jnp....]
    lt x32 -> x0, other arithmetic: 17.6 us -> none  [attend(): positions < length]
  transfers between devices with their start and end apart: 2 -> 0, of which waited for: 2 -> 0; matrix products, arithmetic and copies ran while one was open for 1% -> 0% of each run, Pallas kernels for 0% -> 0%
where the time goes in v2:
time: 58.5 us; the launch traced here: 57.6 us
  Pallas kernels  54.5 us (93%)
  local copies, waits for them, and re-layouts  2.47 us (4%)
  between operations  0.65 us (1%)
    pallas_call x1, Pallas kernels, body(): pl.pallas_call(kernel, out_shape=(jax.ShapeDtypeStruct((ROWS, HD), jnp.bf...  54.5 us
    reshape x1, local copies, waits for them, and re-layouts, body(): moved = moved.reshape(HEADS, 2, BLOCK, 2, HD)  1.76 us

profile of v2, /device:TPU:1, one launch (start us, length us, event | category | flops | bytes accessed | tf_op | source)
XLA Modules:
  0.0 57.6 jit_solution(10000017677883640417)
XLA Ops:
  0.6 54.5 %stretch_attention.1 = (bf16[1024,128]{1,0:T(8,128)(2,1)}, bf16[8,64,128]{2,1,0:T(8,128)(2,1)}) custom-call(s32[32]{0:T(128)} %lens.1, s32[8]{0:T(128)} %bitcast.19, bf16[1024,128]{1,0:T(8,128)(2,1)} %bitcast.13, bf16[1024,128]{1,0:T(8,128)(2,1)} %bitcast.14, bf16[256,128]{1,0:T(8,128)(2,1)} %bitcast.18), custom_call_target="tpu_custom_call" | custom-call | tf_op jit(solution)/shard_map/stretch_attention/pallas_call | solution.py:485
  55.1 0.0 copy-start
  55.1 1.8 %copy.10 = bf16[8,2,16,2,128]{4,0,3,2,1:T(8,128)(2,1)} copy(bf16[8,2,16,2,128]{4,3,2,1,0:T(2,128)(2,1)} %bitcast.17) | data formatting | bytes 262144 | tf_op jit(solution)/shard_map/reshape | solution.py:538
  56.9 0.0 copy-done
  56.9 0.7 %copy.12 = bf16[128,1,8,128]{3,2,1,0:T(8,128)(2,1)} copy(bf16[128,1,8,128]{3,2,1,0:T(8,128)(2,1)S(1)} %bitcast.15) | data formatting | bytes 524288
Async XLA Ops:
  55.1 1.8 %copy-start = (bf16[1024,128]{1,0:T(8,128)(2,1)S(1)}, bf16[1024,128]{1,0:T(8,128)(2,1)}, u32[]{:S(2)}) copy-start(bf16[1024,128]{1,0:T(8,128)(2,1)} %get-tuple-element.4) | copy-start | bytes 786436

commit v3 on v2

--- a/solution.py
+++ b/solution.py
@@ -21,8 +21,7 @@
 OWN = CACHE // PIECE
 MSGS = 14
 PIECES = OWN + 2 * MSGS
-PER_STEP = 8
-STEP = PER_STEP * PIECE
+MOST = 8
 TILE = 512
 BLOCK = 16
 PAGES = TOK // BLOCK
@@ -38,26 +37,17 @@
     return OWN + 2 * m + (0 if forward else 1)
 
 
+def quarter_of(m, forward):
+    return (m + (0 if forward else 2)) % OWN
+
+
 def shard_of(m, forward):
-    if m < 12:
-        hop, quarter = 1 + m // OWN, m % OWN
-    else:
-        hop, quarter = 4, (m - 12 if forward else m - 10)
-    return (-hop if forward else hop), quarter
-
-
-def next_message(m, forward):
-    if m < 8:
-        return m + 4
-    if forward and m in (8, 9):
-        return m + 4
-    if not forward and m in (10, 11):
-        return m + 2
-    return None
+    hop = 1 + m // OWN
+    return (-hop if forward else hop), quarter_of(m, forward)
 
 
 def kernel(lens, plan, q_in, cache_in, fresh_in, out, moved,
-           kv, st, live, qs, acc, top, sbuf, raw, fraw, wide, packed, osend, lsend, oget, lget,
+           kv, st, live, qs, acc, top, sbuf, raw, fraw, wide, packed, landed, paged, osend, lsend, oget, lget,
            in_s, kv_s, kv_r, st_s, st_r, sh_s, sh_r, q_s, q_r, o_s, o_r, l_s, l_r, mg_s, mg_r, own_s):
     ctx = lax.axis_index("ctx")
     head = lax.axis_index("head")
@@ -90,11 +80,7 @@
         pl.semaphore_signal(barrier, inc=1, device_id=peer, device_id_type=MESH)
 
     def kv_copy(m, forward):
-        if m < OWN:
-            src = m
-        else:
-            before = [b for b in range(MSGS) if next_message(b, forward) == m]
-            src = piece_of(before[0], forward)
+        src = quarter_of(m, forward) if m < OWN else piece_of(m - OWN, forward)
         dst = piece_of(m, forward)
         return pltpu.make_async_remote_copy(
             src_ref=kv.at[src],
@@ -105,12 +91,15 @@
             device_id_type=MESH,
         )
 
-    def pass_on(m):
-        for forward in (True, False):
-            kv_copy(m, forward).wait_recv()
-            later = next_message(m, forward)
-            if later is not None:
-                kv_copy(later, forward).start()
+    def arrive(*messages):
+        for m in messages:
+            for forward in (True, False):
+                kv_copy(m, forward).wait_recv()
+
+    def pass_on(*messages):
+        for m in messages:
+            for forward in (True, False):
+                kv_copy(m + OWN, forward).start()
 
     def q_copy(n):
         half = (0, 1, 0, 1, 0, 1)[n]
@@ -174,7 +163,7 @@
         to = (me + d) % HEADS
         return pltpu.make_async_remote_copy(
             src_ref=packed.at[(to % NI) * NH + to // NI],
-            dst_ref=moved.at[dst],
+            dst_ref=landed.at[dst],
             send_sem=mg_s.at[d],
             recv_sem=mg_r.at[d],
             device_id=at_head(to),
@@ -182,7 +171,7 @@
         )
 
     def own_pages():
-        return pltpu.make_async_copy(packed.at[inst * NH + head], moved.at[me], own_s)
+        return pltpu.make_async_copy(packed.at[inst * NH + head], landed.at[me], own_s)
 
     def o_copies(n):
         to = at_y((1, -1, 1, 1, -1, -1)[n])
@@ -214,15 +203,7 @@
 
     first = own_piece(0, None)
     pl.semaphore_wait(barrier, len(peers))
-    for forward in (True, False):
-        kv_copy(0, forward).start()
-    q_copy(0).start()
-    q_copy(2).start()
-    for n in range(1, OWN):
-        own_piece(n, first)
-        for forward in (True, False):
-            kv_copy(n, forward).start()
-
+    kv_copy(0, True).start()
     loads[OWN].wait()
     fresh = fraw[...].astype(jnp.float32)
     wide[OWN] = fresh
@@ -238,8 +219,16 @@
     def _():
         stay_copy().start()
 
-    q_copy(1).start()
-    q_copy(3).start()
+    for n in (0, 2, 1, 3):
+        q_copy(n).start()
+    own_piece(2, first)
+    kv_copy(0, False).start()
+    own_piece(1, first)
+    kv_copy(1, True).start()
+    own_piece(3, first)
+    kv_copy(1, False).start()
+    for forward in (True, False):
+        kv_copy(2, forward).start()
 
     def empty(n, carry):
         acc[:, pl.ds(pl.multiple_of(n * TILE, TILE), TILE)] = jnp.zeros((HD + SUMS, TILE), jnp.float32)
@@ -272,6 +261,19 @@
         page_copy(d, me).start()
     own_pages().start()
 
+    @pl.when(z % NY != 0)
+    def _():
+        shift_copy().wait_recv()
+
+    @pl.when(z % NY == 0)
+    def _():
+        stay_copy().wait()
+
+    for forward in (True, False):
+        st_copy(1, forward, True).start()
+    for forward in (True, False):
+        kv_copy(3, forward).start()
+
     def columns(a, half):
         return pl.ds(pl.multiple_of(a * ROWS + half * TILE, TILE), TILE)
 
@@ -283,97 +285,100 @@
         acc[:, cols] = acc[:, cols] * jnp.exp2(before - peak) + part
         top[:, cols] = peak
 
-    def score(a, half, step, slot):
-        keys = kv[pl.ds(step * PER_STEP, PER_STEP), pl.ds(0, PIECE), :].reshape(STEP, HD)
-        sbuf[slot] = lax.dot_general(keys, qs[columns(a, half), :], NT, preferred_element_type=jnp.float32)
-
-    def weigh(a, half, step, slot):
-        vals = jnp.concatenate([kv[step * PER_STEP + n, pl.ds(PIECE, HD), :] for n in range(PER_STEP)], axis=1)
-        sums = live[:, pl.ds(pl.multiple_of(step * STEP, STEP), STEP)]
-        add(columns(a, half), sbuf[slot], jnp.concatenate([vals, sums], axis=0))
-
-    def turn(n):
-        return jnp.where(n < 4, n, (n + 1) % 4), n // 4
+    def score(a, half, start, count, slot):
+        keys = kv[pl.ds(start, count), pl.ds(0, PIECE), :].reshape(count * PIECE, HD)
+        sbuf[slot, pl.ds(0, count * PIECE), :] = lax.dot_general(
+            keys, qs[columns(a, half), :], NT, preferred_element_type=jnp.float32
+        )
+
+    def weigh(a, half, start, count, slot):
+        vals = jnp.concatenate([kv[start + n, pl.ds(PIECE, HD), :] for n in range(count)], axis=1)
+        sums = live[:, pl.ds(pl.multiple_of(start * PIECE, PIECE), count * PIECE)]
+        scores = sbuf[slot, pl.ds(0, count * PIECE), :]
+        add(columns(a, half), scores, jnp.concatenate([vals, sums], axis=0))
+
+    first_turns = (
+        ((0, 0, 0), (0, 1, 0)),
+        ((1, 0, 0), (2, 0, 0)),
+        ((1, 1, 0), (2, 1, 0)),
+        ((1, 0, 8), (1, 1, 8)),
+        ((2, 0, 8), (2, 1, 8)),
+        ((3, 0, 0), (3, 1, 0)),
+        ((3, 0, 8), (3, 1, 8)),
+    )
+    second_turns = tuple(((a, 0, start), (a, 1, start)) for start in (16, 20) for a in (3, 1, 2))
+    own_turns = tuple(((0, 0, start), (0, 1, start)) for start in (8, 16, 24))
 
     def event_0():
         q_copy(2).wait_recv()
+
+    def event_1():
+        q_copy(0).wait_recv()
+        q_copy(4).start()
+        next_stretch(1)
+        arrive(2)
         pass_on(2)
-
-    def event_1():
         q_copy(3).wait_recv()
         q_copy(5).start()
-        q_copy(0).wait_recv()
-        q_copy(4).start()
+        arrive(3)
         pass_on(3)
-
-        @pl.when(z % NY != 0)
-        def _():
-            shift_copy().wait_recv()
-
-        @pl.when(z % NY == 0)
-        def _():
-            stay_copy().wait()
-
-        for forward in (True, False):
-            st_copy(1, forward, True).start()
 
     def event_2():
         q_copy(1).wait_recv()
+        arrive(4, 5)
+
+    def event_4():
+        next_stretch(2)
+        pass_on(4, 5)
         q_copy(4).wait_recv()
-        pass_on(4)
-
-    def event_3():
         q_copy(5).wait_recv()
-        pass_on(5)
-
-    def event_4():
-        next_stretch(1)
-        pass_on(6)
-
-    def event_5():
-        pass_on(7)
-
-    def event_6():
-        pass_on(8)
-
-    def event_7():
-        next_stretch(2)
-        pass_on(9)
-
-    def event_8():
-        pass_on(10)
-
-    def event_9():
-        pass_on(11)
-
-    def event_10():
+
+    def turns(table, count, events):
+        def tile(n, u):
+            found = [jnp.int32(value) for value in table[0][u]]
+            for when in range(1, len(table)):
+                found = [jnp.where(n == when, value, old) for value, old in zip(table[when][u], found)]
+            return found
+
+        def one_turn(n, carry):
+            for when, event in events.items():
+                pl.when(n == when)(event)
+            one, two, after = tile(n, 0), tile(n, 1), tile(n + 1, 0)
+            score(*two, count, 1)
+            weigh(*one, count, 0)
+            score(*after, count, 0)
+            weigh(*two, count, 1)
+            return carry
+
+        score(*table[0][0], count, 0)
+        lax.fori_loop(0, len(table) - 1, one_turn, 0)
+        one, two = table[-1]
+        score(*two, count, 1)
+        weigh(*one, count, 0)
+        weigh(*two, count, 1)
+
+    arrive(0, 1)
+    pass_on(0, 1)
+    loads[OWN + 1].wait()
+    turns(first_turns, 8, {0: event_0, 1: event_1, 2: event_2, 4: event_4})
+    arrive(6, 7)
+
+    def event_second_0():
         next_stretch(3)
-
-    events = (
-        event_0, event_1, event_2, event_3, event_4, event_5, event_6, event_7, event_8, event_9, event_10,
-    )
-    pass_on(0)
-    pass_on(1)
-    loads[OWN + 1].wait()
-    score(0, 0, 0, 0)
-    last = 11
-
-    def one_turn(n, carry):
-        for when, event in enumerate(events):
-            pl.when(n == when)(event)
-        a, step = turn(n)
-        after, step_after = turn(n + 1)
-        score(a, 1, step, 1)
-        weigh(a, 0, step, 0)
-        score(after, 0, step_after, 0)
-        weigh(a, 1, step, 1)
-        return carry
-
-    lax.fori_loop(0, last, one_turn, 0)
-    a, step = turn(last)
-    score(a, 1, step, 1)
-    weigh(a, 0, step, 0)
-    weigh(a, 1, step, 1)
+        pass_on(6, 7)
+
+    def event_second_2():
+        arrive(8, 9)
+        pass_on(8, 9)
+
+    turns(second_turns, 4, {0: event_second_0, 2: event_second_2})
+
+    for d in range(1, HEADS):
+        page_copy(d, (me - d + HEADS) % HEADS).wait_recv()
+    own_pages().wait()
+    for h in range(HEADS):
+        paged[pl.ds(h, 4 * BLOCK, stride=HEADS), :] = landed[h].astype(jnp.float32)
+    moved[...] = paged[...].astype(jnp.bfloat16)
 
     def stretch(a, row):
         pairs = [(j - y + NY) % NY for j in range(row + 1)]
@@ -432,25 +437,23 @@
         for copy in o_copies(n):
             copy.start()
 
-    pass_on(12)
-    pass_on(13)
-    order = (3, 1, 2, 0)
-    score(order[0], 0, 3, 0)
-    for n, a in enumerate(order):
-        score(a, 1, 3, 1)
-        weigh(a, 0, 3, 0)
-        if n < 3:
-            score(order[n + 1], 0, 3, 0)
-        weigh(a, 1, 3, 1)
-        if a == 3:
+    arrive(10, 11, 12, 13)
+    order = ((3, 0), (3, 1), (1, 1), (2, 0), (1, 0), (2, 1))
+    score(*order[0], 24, 8, 0)
+    for n, (a, half) in enumerate(order):
+        if n + 1 < len(order):
+            score(*order[n + 1], 24, 8, (n + 1) % 2)
+        weigh(a, half, 24, 8, n % 2)
+        if n == 1:
             send(0, *finish(3, 0))
             send(1, *finish(3, 1))
-        if a == 1:
+        if n == 3:
             send(3, *finish(1, 1))
-        if a == 2:
             send(4, *finish(2, 0))
+        if n == 5:
             send(2, *join([finish(1, 0), arrived(0)]))
             send(5, *join([finish(2, 1), arrived(1)]))
+    turns(own_turns, 8, {})
     stretch_of(0)
 
     for half in (0, 1):
@@ -475,8 +478,6 @@
             copy.wait_send()
     for d in range(1, HEADS):
         page_copy(d, me).wait_send()
-        page_copy(d, (me - d + HEADS) % HEADS).wait_recv()
-    own_pages().wait()
 
 
 def body(queries, cache_kv, new_kv, cache_lengths, plan):
@@ -486,10 +487,10 @@
         kernel,
         out_shape=(
             jax.ShapeDtypeStruct((ROWS, HD), jnp.bfloat16),
-            jax.ShapeDtypeStruct((HEADS, 4 * BLOCK, HD), jnp.bfloat16),
+            jax.ShapeDtypeStruct((4 * BLOCK * HEADS, HD), jnp.bfloat16),
         ),
         in_specs=[smem, smem, hbm, hbm, hbm],
-        out_specs=(pl.BlockSpec(memory_space=pltpu.VMEM), pl.BlockSpec(memory_space=pl.ANY)),
+        out_specs=(pl.BlockSpec(memory_space=pltpu.VMEM),) * 2,
         scratch_shapes=[
             pltpu.VMEM((PIECES, PIECE + HD, HD), jnp.bfloat16),
             pltpu.VMEM((NZ + 1, TOK + HD, HD), jnp.bfloat16),
@@ -497,11 +498,13 @@
             pltpu.VMEM((NY * ROWS, HD), jnp.bfloat16),
             pltpu.VMEM((HD + SUMS, NY * ROWS), jnp.float32),
             pltpu.VMEM((1, NY * ROWS), jnp.float32),
-            pltpu.VMEM((2, STEP, TILE), jnp.float32),
+            pltpu.VMEM((2, MOST * PIECE, TILE), jnp.float32),
             pltpu.VMEM((OWN, 2 * PIECE, HD), jnp.bfloat16),
             pltpu.VMEM((2 * TOK, HD), jnp.bfloat16),
             pltpu.VMEM((OWN + 1, 2 * PIECE, HD), jnp.float32),
             pltpu.VMEM((HEADS, 4 * BLOCK, HD), jnp.bfloat16),
+            pltpu.VMEM((HEADS, 4 * BLOCK, HD), jnp.bfloat16),
+            pltpu.VMEM((4 * BLOCK * HEADS, HD), jnp.float32),
             pltpu.VMEM((6, HD, TILE), jnp.bfloat16),
             pltpu.VMEM((6, 1, TILE), jnp.float32),
             pltpu.VMEM((6, HD, TILE), jnp.bfloat16),
@@ -524,19 +527,20 @@
             pltpu.SemaphoreType.DMA,
         ],
         compiler_params=pltpu.CompilerParams(
-            collective_id=0, has_side_effects=True, vmem_limit_bytes=58 * 2 ** 20
+            collective_id=0, has_side_effects=True, vmem_limit_bytes=32 * 2 ** 20
         ),
         name="stretch_attention",
     )(
         cache_lengths,
         plan.reshape(PAGES),
-        queries.reshape(ROWS, HD),
-        cache_kv.reshape(2 * CACHE, HD),
-        new_kv.reshape(2 * TOK, HD),
+        *(pltpu.with_memory_space_constraint(x, pltpu.HBM) for x in (
+            queries.reshape(ROWS, HD),
+            cache_kv.reshape(2 * CACHE, HD),
+            new_kv.reshape(2 * TOK, HD),
+        )),
     )
     attended = out.reshape(TOK, 1, GROUP, HD)
-    moved = moved.reshape(HEADS, 2, BLOCK, 2, HD)
-    migrated = jnp.transpose(moved, (1, 2, 3, 0, 4)).reshape(1, 1, 2, BLOCK, 2, HEADS, HD)
+    migrated = moved.reshape(1, 1, 2, BLOCK, 2, HEADS, HD)
     return attended, migrated
 
 

time: 58.5 us -> 55.3 us (0.945)
  the two profiles are of different devices: /device:TPU:1 before, /device:TPU:24 now
where the time goes in v3:
time: 55.3 us; the launch traced here: 55.2 us
  Pallas kernels  52.5 us (95%)
  local copies, waits for them, and re-layouts  2.02 us (4%)
  between operations  0.66 us (1%)
    pallas_call x1, Pallas kernels, body(): pl.pallas_call(kernel, out_shape=(jax.ShapeDtypeStruct((ROWS, HD), jnp.bf...  52.5 us
    unnamed x6, local copies, waits for them, and re-layouts  2.02 us

profile of v3, /device:TPU:24, one launch (start us, length us, event | category | flops | bytes accessed | tf_op | source)
XLA Modules:
  0.0 55.2 jit_solution(14405642765445239440)
XLA Ops:
  0.6 0.0 copy-start
  0.6 0.0 copy-start.1
  0.7 0.6 %copy-done = s32[32]{0:T(128)S(1)} copy-done((s32[32]{0:T(128)S(1)}, s32[32]{0:T(128)}, u32[]{:S(2)}) %copy-start) | copy-done | bytes 152
  1.3 0.0 copy-done.1
  1.3 52.5 %stretch_attention.1 = (bf16[1024,128]{1,0:T(8,128)(2,1)S(1)}, bf16[512,128]{1,0:T(8,128)(2,1)S(1)}) custom-call(s32[32]{0:T(128)S(1)} %copy-done, s32[8]{0:T(128)S(1)} %bitcast.10, bf16[1024,128]{1,0:T(8,128)(2,1)} %bitcast.11, bf16[1024,128]{1,0:T(8,128)(2,1)} %bitcast.12, bf16[256,128]{1,0:T(8,128)(2,1)} %bitcast.13), custom_call_target="tpu_custom_call" | custom-call | tf_op jit(solution)/shard_map/stretch_attention/pallas_call | solution.py:486
  53.8 0.7 %copy.10 = bf16[128,1,8,128]{3,2,1,0:T(8,128)(2,1)} copy(bf16[128,1,8,128]{3,2,1,0:T(8,128)(2,1)S(1)} %bitcast.8) | data formatting | bytes 524288
  54.5 0.7 %copy.11 = bf16[1,1,2,16,2,8,128]{6,5,4,3,2,1,0:T(8,128)(2,1)} copy(bf16[1,1,2,16,2,8,128]{6,5,4,3,2,1,0:T(8,128)(2,1)S(1)} %bitcast.9) | data formatting | bytes 262144
Async XLA Ops:
  0.6 0.7 %copy-start = (s32[32]{0:T(128)S(1)}, s32[32]{0:T(128)}, u32[]{:S(2)}) copy-start(s32[32]{0:T(128)} %lens.1) | copy-start | bytes 388
  0.6 0.7 %copy-start.1 = (s32[8,1]{0,1:T(1,128)S(1)}, s32[8,1]{0,1:T(1,128)}, u32[]{:S(2)}) copy-start(s32[8,1]{0,1:T(1,128)} %param.9) | copy-start | bytes 100

commit v4 on v3

--- a/solution.py
+++ b/solution.py
@@ -70,14 +70,15 @@
     ]
     loads.append(pltpu.make_async_copy(fresh_in, fraw, in_s.at[OWN]))
     loads.append(pltpu.make_async_copy(q_in, qs.at[pl.ds(0, ROWS)], in_s.at[OWN + 1]))
-    for load in loads:
-        load.start()
+    loads[0].start()
 
     barrier = pltpu.get_barrier_semaphore()
     peers = [at_z(1), at_z(-1), at_y(1), at_y(2), at_y(3)]
     peers += [at_head((me + d) % HEADS) for d in range(1, HEADS)]
     for peer in peers:
         pl.semaphore_signal(barrier, inc=1, device_id=peer, device_id_type=MESH)
+    for n in (OWN, 2, 1, 3, OWN + 1):
+        loads[n].start()
 
     def kv_copy(m, forward):
         src = quarter_of(m, forward) if m < OWN else piece_of(m - OWN, forward)
@@ -301,13 +302,15 @@
         ((0, 0, 0), (0, 1, 0)),
         ((1, 0, 0), (2, 0, 0)),
         ((1, 1, 0), (2, 1, 0)),
+    )
+    more_turns = (
         ((1, 0, 8), (1, 1, 8)),
         ((2, 0, 8), (2, 1, 8)),
         ((3, 0, 0), (3, 1, 0)),
         ((3, 0, 8), (3, 1, 8)),
     )
-    second_turns = tuple(((a, 0, start), (a, 1, start)) for start in (16, 20) for a in (3, 1, 2))
-    own_turns = tuple(((0, 0, start), (0, 1, start)) for start in (8, 16, 24))
+    def whole(start, *shards):
+        return tuple(((a, 0, start), (a, 1, start)) for a in shards)
 
     def event_0():
         q_copy(2).wait_recv()
@@ -320,12 +323,9 @@
         pass_on(2)
         q_copy(3).wait_recv()
         q_copy(5).start()
+        q_copy(1).wait_recv()
         arrive(3)
         pass_on(3)
-
-    def event_2():
-        q_copy(1).wait_recv()
-        arrive(4, 5)
 
     def event_4():
         next_stretch(2)
@@ -360,25 +360,20 @@
     arrive(0, 1)
     pass_on(0, 1)
     loads[OWN + 1].wait()
-    turns(first_turns, 8, {0: event_0, 1: event_1, 2: event_2, 4: event_4})
+    turns(first_turns, 8, {0: event_0, 1: event_1})
+    turns(whole(8, 0), 4, {})
+    arrive(4, 5)
+    turns(more_turns, 8, {1: event_4})
     arrive(6, 7)
 
-    def event_second_0():
+    def event_third():
         next_stretch(3)
         pass_on(6, 7)
 
-    def event_second_2():
-        arrive(8, 9)
-        pass_on(8, 9)
-
-    turns(second_turns, 4, {0: event_second_0, 2: event_second_2})
-
-    for d in range(1, HEADS):
-        page_copy(d, (me - d + HEADS) % HEADS).wait_recv()
-    own_pages().wait()
-    for h in range(HEADS):
-        paged[pl.ds(h, 4 * BLOCK, stride=HEADS), :] = landed[h].astype(jnp.float32)
-    moved[...] = paged[...].astype(jnp.bfloat16)
+    turns(whole(16, 3, 1, 2), 4, {1: event_third})
+    arrive(8, 9)
+    pass_on(8, 9)
+    turns(whole(20, 3, 1, 2), 4, {})
 
     def stretch(a, row):
         pairs = [(j - y + NY) % NY for j in range(row + 1)]
@@ -405,11 +400,16 @@
 
     next_stretch(4)
 
+    def third_step():
+        arrive(10, 11)
+        turns(whole(24, 3), 4, {})
+
     def stretch_turn(n, carry):
-        stretch_of(jnp.where(n == 0, 3, n))
+        pl.when(n == 1)(third_step)
+        stretch_of(jnp.where(n == 0, 3, 1))
         return carry
 
-    lax.fori_loop(0, 3, stretch_turn, 0)
+    lax.fori_loop(0, 2, stretch_turn, 0)
 
     def finish(a, half):
         cols = columns(a, half)
@@ -437,27 +437,40 @@
         for copy in o_copies(n):
             copy.start()
 
-    arrive(10, 11, 12, 13)
-    order = ((3, 0), (3, 1), (1, 1), (2, 0), (1, 0), (2, 1))
+    arrive(12, 13)
+    turns(whole(28, 3), 4, {})
+    for half in (0, 1):
+        send(half, *finish(3, half))
+    stretch_of(2)
+    order = ((1, 1), (2, 0), (1, 0), (2, 1))
     score(*order[0], 24, 8, 0)
     for n, (a, half) in enumerate(order):
         if n + 1 < len(order):
             score(*order[n + 1], 24, 8, (n + 1) % 2)
         weigh(a, half, 24, 8, n % 2)
         if n == 1:
-            send(0, *finish(3, 0))
-            send(1, *finish(3, 1))
-        if n == 3:
             send(3, *finish(1, 1))
             send(4, *finish(2, 0))
-        if n == 5:
-            send(2, *join([finish(1, 0), arrived(0)]))
-            send(5, *join([finish(2, 1), arrived(1)]))
-    turns(own_turns, 8, {})
+    send(2, *join([finish(1, 0), arrived(0)]))
+    send(5, *join([finish(2, 1), arrived(1)]))
+    turns(whole(12, 0), 4, {})
+    turns(whole(16, 0) + whole(24, 0), 8, {})
     stretch_of(0)
 
+    for d in range(1, HEADS):
+        page_copy(d, (me - d + HEADS) % HEADS).wait_recv()
+    own_pages().wait()
+    for h in range(HEADS):
+        paged[pl.ds(h, 4 * BLOCK, stride=HEADS), :] = landed[h].astype(jnp.float32)
+    moved[...] = paged[...].astype(jnp.bfloat16)
+
+    levels = []
     for half in (0, 1):
-        result, _ = join([finish(0, half), arrived(2 + half), arrived(4 + half)])
+        result, level = join([finish(0, half), arrived((4, 3)[half])])
+        acc[pl.ds(0, HD), columns(0, half)] = result
+        levels.append(level)
+    for half in (0, 1):
+        result, _ = join([(acc[pl.ds(0, HD), columns(0, half)], levels[half]), arrived((2, 5)[half])])
         out[pl.ds(half * TILE, TILE), :] = result.T.astype(jnp.bfloat16)
 
     for m in range(MSGS):
@@ -531,9 +544,9 @@
         ),
         name="stretch_attention",
     )(
-        cache_lengths,
-        plan.reshape(PAGES),
         *(pltpu.with_memory_space_constraint(x, pltpu.HBM) for x in (
+            cache_lengths,
+            plan.reshape(PAGES),
             queries.reshape(ROWS, HD),
             cache_kv.reshape(2 * CACHE, HD),
             new_kv.reshape(2 * TOK, HD),

time: 55.3 us -> 51.5 us (0.931)
  the two profiles are of different devices: /device:TPU:24 before, /device:TPU:1 now
where the time goes in v4:
time: 51.5 us; the launch traced here: 51 us
  Pallas kernels  49 us (95%)
  local copies, waits for them, and re-layouts  1.36 us (3%)
  between operations  0.64 us (1%)
    pallas_call x1, Pallas kernels, body(): pl.pallas_call(kernel, out_shape=(jax.ShapeDtypeStruct((ROWS, HD), jnp.bf...  49 us
    unnamed x2, local copies, waits for them, and re-layouts  1.36 us

profile of v4, /device:TPU:1, one launch (start us, length us, event | category | flops | bytes accessed | tf_op | source)
XLA Modules:
  0.0 51.0 jit_solution(18019319887536884059)
XLA Ops:
  0.6 49.0 %stretch_attention.1 = (bf16[1024,128]{1,0:T(8,128)(2,1)S(1)}, bf16[512,128]{1,0:T(8,128)(2,1)S(1)}) custom-call(s32[32]{0:T(128)} %lens.1, s32[8]{0:T(128)} %bitcast.13, bf16[1024,128]{1,0:T(8,128)(2,1)} %bitcast.10, bf16[1024,128]{1,0:T(8,128)(2,1)} %bitcast.11, bf16[256,128]{1,0:T(8,128)(2,1)} %bitcast.12), custom_call_target="tpu_custom_call" | custom-call | tf_op jit(solution)/shard_map/stretch_attention/pallas_call | solution.py:499
  49.6 0.7 %copy.10 = bf16[128,1,8,128]{3,2,1,0:T(8,128)(2,1)} copy(bf16[128,1,8,128]{3,2,1,0:T(8,128)(2,1)S(1)} %bitcast.8) | data formatting | bytes 524288
  50.3 0.7 %copy.11 = bf16[1,1,2,16,2,8,128]{6,5,4,3,2,1,0:T(8,128)(2,1)} copy(bf16[1,1,2,16,2,8,128]{6,5,4,3,2,1,0:T(8,128)(2,1)S(1)} %bitcast.9) | data formatting | bytes 262144

commit v5 on v4

--- a/solution.py
+++ b/solution.py
@@ -491,6 +491,20 @@
             copy.wait_send()
     for d in range(1, HEADS):
         page_copy(d, me).wait_send()
+
+
+def write(out_in, moved_in, out, moved, sems):
+    copies = [
+        pltpu.make_async_copy(out_in.at[pl.ds(n * 256, 256)], out.at[pl.ds(n * 256, 256)], sems.at[n]) for n in range(4)
+    ]
+    copies += [
+        pltpu.make_async_copy(moved_in.at[pl.ds(n * 256, 256)], moved.at[pl.ds(n * 256, 256)], sems.at[4 + n])
+        for n in range(2)
+    ]
+    for copy in copies:
+        copy.start()
+    for copy in copies:
+        copy.wait()
 
 
 def body(queries, cache_kv, new_kv, cache_lengths, plan):
@@ -552,6 +566,18 @@
             new_kv.reshape(2 * TOK, HD),
         )),
     )
+    vmem = pl.BlockSpec(memory_space=pltpu.VMEM)
+    out, moved = pl.pallas_call(
+        write,
+        out_shape=(
+            jax.ShapeDtypeStruct((ROWS, HD), jnp.bfloat16),
+            jax.ShapeDtypeStruct((4 * BLOCK * HEADS, HD), jnp.bfloat16),
+        ),
+        in_specs=[vmem, vmem],
+        out_specs=(hbm, hbm),
+        scratch_shapes=[pltpu.SemaphoreType.DMA((6,))],
+        name="write_results",
+    )(*(pltpu.with_memory_space_constraint(x, pltpu.VMEM) for x in (out, moved)))
     attended = out.reshape(TOK, 1, GROUP, HD)
     migrated = moved.reshape(1, 1, 2, BLOCK, 2, HEADS, HD)
     return attended, migrated

time: 51.5 us -> 51.1 us (level)
  local copies, waits for them, and re-layouts: 1.36 us -> 0 us
  Pallas kernels: 49 us -> 49.8 us
    unnamed x2 -> x0, local copies, waits for them, and re-layouts: 1.36 us -> none
    pallas_call x0 -> x1, Pallas kernels: none -> 0.79 us  [body(): pl.pallas_call(write, out_shape=(jax.ShapeDtypeStruct((ROWS, HD), jnp.bfl...]
where the time goes in v5:
time: 51.1 us; the launch traced here: 50.6 us
  Pallas kernels  49.8 us (97%)
  between operations  0.82 us (2%)
    pallas_call x1, Pallas kernels, body(): pl.pallas_call(kernel, out_shape=(jax.ShapeDtypeStruct((ROWS, HD), jnp.bf...  49 us

profile of v5, /device:TPU:1, one launch (start us, length us, event | category | flops | bytes accessed | tf_op | source)
XLA Modules:
  0.0 50.6 jit_solution(2379988427992034027)
XLA Ops:
  0.6 49.0 %stretch_attention.1 = (bf16[1024,128]{1,0:T(8,128)(2,1)S(1)}, bf16[512,128]{1,0:T(8,128)(2,1)S(1)}) custom-call(s32[32]{0:T(128)} %lens.1, s32[8]{0:T(128)} %bitcast.11, bf16[1024,128]{1,0:T(8,128)(2,1)} %bitcast.8, bf16[1024,128]{1,0:T(8,128)(2,1)} %bitcast.9, bf16[256,128]{1,0:T(8,128)(2,1)} %bitcast.10), custom_call_target="tpu_custom_call" | custom-call | tf_op jit(solution)/shard_map/stretch_attention/pallas_call | solution.py:513
  49.6 0.8 %write_results.1 = (bf16[1024,128]{1,0:T(8,128)(2,1)}, bf16[512,128]{1,0:T(8,128)(2,1)}) custom-call(bf16[1024,128]{1,0:T(8,128)(2,1)S(1)} %get-tuple-element.6.out_in, bf16[512,128]{1,0:T(8,128)(2,1)S(1)} %get-tuple-element.7.moved_in), custom_call_target="tpu_custom_call" | custom-call | tf_op jit(solution)/shard_map/write_results/pallas_call | solution.py:570

commit v6 on v5

--- a/solution.py
+++ b/solution.py
@@ -194,7 +194,7 @@
 
     def own_piece(n, first):
         loads[n].wait()
-        wide[n] = raw[n].astype(jnp.float32)
+        wide[n, pl.ds(0, 2 * PIECE), :] = raw[n].astype(jnp.float32)
         keys, values = split(n)
         first = keys[0:1, :] if n == 0 else first
         usable = lax.broadcasted_iota(jnp.int32, (PIECE, HD), 0) + n * PIECE < length
@@ -207,7 +207,7 @@
     kv_copy(0, True).start()
     loads[OWN].wait()
     fresh = fraw[...].astype(jnp.float32)
-    wide[OWN] = fresh
+    wide[OWN, pl.ds(0, 2 * TOK), :] = fresh
     keys, values = split(OWN)
     st[NZ, pl.ds(0, TOK), :] = keys.astype(jnp.bfloat16)
     st[NZ, pl.ds(TOK, HD), :] = values.T.astype(jnp.bfloat16)
@@ -462,7 +462,7 @@
     own_pages().wait()
     for h in range(HEADS):
         paged[pl.ds(h, 4 * BLOCK, stride=HEADS), :] = landed[h].astype(jnp.float32)
-    moved[...] = paged[...].astype(jnp.bfloat16)
+    moved[...] = paged[pl.ds(0, 4 * BLOCK * HEADS), :].astype(jnp.bfloat16)
 
     levels = []
     for half in (0, 1):
@@ -528,10 +528,10 @@
             pltpu.VMEM((2, MOST * PIECE, TILE), jnp.float32),
             pltpu.VMEM((OWN, 2 * PIECE, HD), jnp.bfloat16),
             pltpu.VMEM((2 * TOK, HD), jnp.bfloat16),
-            pltpu.VMEM((OWN + 1, 2 * PIECE, HD), jnp.float32),
+            pltpu.VMEM((OWN + 1, 2 * PIECE + 8, HD), jnp.float32),
             pltpu.VMEM((HEADS, 4 * BLOCK, HD), jnp.bfloat16),
             pltpu.VMEM((HEADS, 4 * BLOCK, HD), jnp.bfloat16),
-            pltpu.VMEM((4 * BLOCK * HEADS, HD), jnp.float32),
+            pltpu.VMEM((4 * BLOCK * HEADS + 8, HD), jnp.float32),
             pltpu.VMEM((6, HD, TILE), jnp.bfloat16),
             pltpu.VMEM((6, 1, TILE), jnp.float32),
             pltpu.VMEM((6, HD, TILE), jnp.bfloat16),

time: 51.1 us -> 51.1 us (level)
  no operation moved by 1% of the time
where the time goes in v6:
time: 51.1 us; the launch traced here: 50.6 us
  Pallas kernels  49.8 us (97%)
  between operations  0.82 us (2%)
    pallas_call x1, Pallas kernels, body(): pl.pallas_call(kernel, out_shape=(jax.ShapeDtypeStruct((ROWS, HD), jnp.bf...  49 us

profile of v6, /device:TPU:1, one launch (start us, length us, event | category | flops | bytes accessed | tf_op | source)
XLA Modules:
  0.0 50.6 jit_solution(16623933054756007306)
XLA Ops:
  0.6 49.0 %stretch_attention.1 = (bf16[1024,128]{1,0:T(8,128)(2,1)S(1)}, bf16[512,128]{1,0:T(8,128)(2,1)S(1)}) custom-call(s32[32]{0:T(128)} %lens.1, s32[8]{0:T(128)} %bitcast.11, bf16[1024,128]{1,0:T(8,128)(2,1)} %bitcast.8, bf16[1024,128]{1,0:T(8,128)(2,1)} %bitcast.9, bf16[256,128]{1,0:T(8,128)(2,1)} %bitcast.10), custom_call_target="tpu_custom_call" | custom-call | tf_op jit(solution)/shard_map/stretch_attention/pallas_call | solution.py:513
  49.6 0.8 %write_results.1 = (bf16[1024,128]{1,0:T(8,128)(2,1)}, bf16[512,128]{1,0:T(8,128)(2,1)}) custom-call(bf16[1024,128]{1,0:T(8,128)(2,1)S(1)} %get-tuple-element.6.out_in, bf16[512,128]{1,0:T(8,128)(2,1)S(1)} %get-tuple-element.7.moved_in), custom_call_target="tpu_custom_call" | custom-call | tf_op jit(solution)/shard_map/write_results/pallas_call | solution.py:570
